TPU v7x, 512 devices: a whole 4x4x16 slice. The times are simulated.
512 devices in a mesh: row: 64 (over z, y), col: 8 (over x, core).
Axes of the slice: x: 4, y: 4, z: 16, core: 2. Of those that a mesh axis runs over, the one named last changes fastest.
Arguments:
- block_vals: bfloat16 [128, 1024, 128], P('row', 'col'), may hold values from -6 to 6
- block_slot: int32 [128, 8], P('row', 'col'), may hold values from 0 to 191, as said below
- block_count: int32 [64, 8], P('row', 'col'), may hold values from 1 to 2, as said below
- omega: bfloat16 [24576, 256], P('col'), may hold values from -6 to 6
Outputs:
- basis: bfloat16 [65536, 256], P(('row', 'col'))
- projected: float32 [8, 3072, 256], P('col', 'row')
- core: float32 [256, 256], replicated
Inputs may be any that keep to these rules, and one draw needn't show every extreme that they name: `block_slot`: within one device's 2 slots each block position appears at most once; position s is row block s // 24 and column block s % 24 of that device's shard. `block_count`: some device has all 2 slots live in every draw.
All inputs are finite; a program needn't handle non-finite values.
Results may differ from a plain program's by a relative error of at most 0.0015.
The roundings to bfloat16 on the way count: a program that leaves them out, or rounds other values in their place, can miss the bound.
Values may be sent and summed in bfloat16 or wider, within the bound.
A program may use at most 64 MiB of HBM per device.

v0:
```python
import jax
import jax.numpy as jnp
from jax import lax
from jax.sharding import PartitionSpec as P

RB = 8


def orthonormalize(rows_here, gram):
    factor = jnp.linalg.cholesky(gram)
    inverse = jax.scipy.linalg.solve_triangular(
        factor, jnp.eye(gram.shape[0], dtype=jnp.float32), lower=True
    )
    return jnp.dot(
        rows_here, inverse.T, precision=lax.Precision.HIGHEST, preferred_element_type=jnp.float32
    ).astype(jnp.bfloat16)


def body(block_vals, block_slot, block_count, omega):
    width = block_vals.shape[1]
    slots_here = block_vals.shape[0]
    rank = omega.shape[1]
    col_blocks = omega.shape[0] // width
    local_rows = RB * width
    total_rows = local_rows * lax.axis_size("row")
    total_cols = omega.shape[0] * lax.axis_size("col")
    slot_ids = block_slot[:, 0]
    row_blk = slot_ids // col_blocks
    col_blk = slot_ids % col_blocks
    live = jnp.arange(slots_here) < block_count[0, 0]
    picked = omega.reshape(col_blocks, width, rank)[col_blk]
    prod = jnp.einsum("bij,bjl->bil", block_vals, picked, preferred_element_type=jnp.float32)
    row_select = ((row_blk[None, :] == jnp.arange(RB)[:, None]) & live[None, :]).astype(jnp.float32)
    partial_value = jnp.einsum(
        "rb,bil->ril", row_select, prod, precision=lax.Precision.HIGHEST
    ).reshape(local_rows, rank)
    sketch = lax.psum(partial_value, "col")
    gram_term = jnp.dot(
        sketch.T, sketch, precision=lax.Precision.HIGHEST, preferred_element_type=jnp.float32
    )
    gram = lax.psum(gram_term, "row") / total_rows
    basis_rows = orthonormalize(sketch, gram)
    share_rows = local_rows // lax.axis_size("col")
    basis_out = lax.dynamic_slice_in_dim(
        basis_rows, lax.axis_index("col") * share_rows, share_rows, 0
    )
    basis_picked = basis_rows.reshape(RB, width, rank)[row_blk]
    col_prod = jnp.einsum(
        "bji,bjl->bil", block_vals, basis_picked, preferred_element_type=jnp.float32
    )
    col_select = ((col_blk[None, :] == jnp.arange(col_blocks)[:, None]) & live[None, :]).astype(
        jnp.float32
    )
    col_partial = jnp.einsum("kb,bil->kil", col_select, col_prod, precision=lax.Precision.HIGHEST)
    col_partial = col_partial.reshape(1, col_blocks * width, rank)
    projected = lax.psum_scatter(col_partial, "row", scatter_dimension=1, tiled=True) / jnp.sqrt(
        jnp.float32(total_rows)
    )
    core_term = jnp.einsum("cil,cim->lm", projected, projected, precision=lax.Precision.HIGHEST)
    core = lax.psum(core_term, ("row", "col")) / total_cols
    return (basis_out, projected, core)


def solution(mesh):
    placed = (P("row", "col", None), P("row", "col"), P("row", "col"), P("col", None))
    return jax.shard_map(
        body,
        mesh=mesh,
        in_specs=placed,
        out_specs=(P(("row", "col"), None), P("col", "row", None), P()),
        check_vma=False,
    )
```

profile of v0, /device:TPU:1, one launch (start us, length us, event | category | flops | bytes accessed | tf_op | source)
XLA Modules:
  0.0 1592.4 jit_solution(4694334502824846960)
XLA Ops:
  8.0 0.7 fusion.29
  8.7 0.7 and_select_fusion.1
  9.4 0.6 gather_fusion
  9.9 1.1 fusion.34
  11.2 0.8 fusion.6
  11.9 1.4 copy.9
  13.4 81.6 %all-reduce.5.cloned.1.call-done = f32[1024,256]{1,0:T(8,128)} async-done(((f32[1024,256]{1,0:T(8,128)}), f32[1024,256]{1,0:T(8,128)}) %all-reduce.5.cloned.1.call-update) | async-done | bytes 1048592 | tf_op jit(solution)/shard_map/psum | solution.py:37
  95.0 4.1 fusion.35
  99.9 252.4 %all-reduce.7.cloned.1.call-done = f32[256,256]{0,1:T(8,128)} async-done(((f32[256,256]{0,1:T(8,128)}), f32[256,256]{0,1:T(8,128)}) %all-reduce.7.cloned.1.call-update) | async-done | bytes 262160 | tf_op jit(solution)/shard_map/psum | solution.py:41
  352.3 1.0 broadcast_multiply_fusion.1
  353.4 1.0 fusion.5
  354.4 11.7 cholesky.50
  366.2 9.8 custom-call.15
  376.5 11.7 cholesky.105
  388.2 0.6 compare_reduce_fusion
  390.2 0.7 triangular_solve.63
  390.9 4.0 while.1
  390.9 0.6 fusion.49
  391.5 1.4 bitcast_dynamic-update-slice_fusion.2
  392.9 0.6 fusion.49
  393.5 1.4 bitcast_dynamic-update-slice_fusion.2
  394.9 19.7 %custom-call.16 = f32[2,128,128]{1,2,0:T(8,128)S(1)} custom-call(f32[2,128,128]{2,1,0:T(8,128)S(1)} %get-tuple-element.10), custom_call_target="InvertDiagBlocksLowerTriangular" | custom-call | tf_op jit(solution)/shard_map/jit(_solve_triangular)/triangular_solve | solution.py:11
  415.4 1.0 convolution_convert_fusion
  416.5 0.6 gather_fusion.1
  417.4 1.6 fusion.3
  419.0 2.6 copy.12
  421.7 691.0 %reduce-scatter.2.cloned.1.call-done = f32[1,48,256]{2,1,0:T(8,128)} async-done(((f32[1,3072,256]{2,1,0:T(8,128)}), f32[1,48,256]{2,1,0:T(8,128)}) %reduce-scatter.2.cloned.1.call-update) | async-done | bytes 49168 | tf_op jit(solution)/shard_map/reduce_scatter | solution.py:56
  1112.7 0.8 broadcast_multiply_fusion.2
  1113.5 1.1 fusion.15
  1114.7 0.6 constant_dynamic-slice_fusion.1
  1115.3 468.8 %all-reduce.9.cloned.1.call-done = f32[256,256]{1,0:T(8,128)} async-done(((f32[256,256]{1,0:T(8,128)}), f32[256,256]{1,0:T(8,128)}) %all-reduce.9.cloned.1.call-update) | async-done | bytes 262160 | tf_op jit(solution)/shard_map/psum | solution.py:60
  1584.2 1.7 broadcast_multiply_fusion
  (38 shorter events, 3.1 us)
Async XLA Ops:
  7.2 2.2 copy-start
  7.2 87.8 %all-reduce.5.cloned.1.call-start = ((), (), s32[]{:S(2)}) async-start(), calls=%async_computation.1 | async-start | bytes 2097152 | tf_op jit(solution)/shard_map/psum | solution.py:37
  13.3 339.0 %all-reduce.7.cloned.1.call-start = ((), (), s32[]{:S(2)}) async-start(), calls=%async_computation.2 | async-start | bytes 524288 | tf_op jit(solution)/shard_map/psum | solution.py:41
  99.0 316.4 %copy-start.1 = (f32[1024,256]{1,0:T(8,128)S(1)}, f32[1024,256]{1,0:T(8,128)}, u32[]{:S(2)}) copy-start(f32[1024,256]{1,0:T(8,128)} %all-reduce.5.cloned.1.call-done) | copy-start | bytes 3145732
  99.1 1013.7 %reduce-scatter.2.cloned.1.call-start = ((), (), s32[]{:S(2)}) async-start(), calls=%async_computation.3 | async-start | bytes 3194880 | tf_op jit(solution)/shard_map/reduce_scatter | solution.py:56
  353.4 63.7 %copy-start.2 = (bf16[2,128,128]{2,1,0:T(8,128)(2,1)S(1)}, bf16[2,128,128]{2,1,0:T(8,128)(2,1)}, u32[]{:S(2)}) copy-start(bf16[2,128,128]{2,1,0:T(8,128)(2,1)} %param.4) | copy-start | bytes 196612
  421.7 1162.5 %all-reduce.9.cloned.1.call-start = ((), (), s32[]{:S(2)}) async-start(), calls=%async_computation.4 | async-start | bytes 524288 | tf_op jit(solution)/shard_map/psum | solution.py:60
  1113.5 472.3 %copy-start.3 = (f32[1,48,256]{2,1,0:T(8,128)}, f32[1,48,256]{2,1,0:T(8,128)S(1)}, u32[]{:S(2)}) copy-start(f32[1,48,256]{2,1,0:T(8,128)S(1)} %broadcast_multiply_fusion.2) | copy-start | bytes 147460
Sparse Core Ops, SparseCore 0:
  13.4 81.4 all-reduce.4
  99.2 253.0 all-reduce.6
  421.8 690.9 reduce-scatter.1
  1119.5 464.6 all-reduce.8
where the time goes:
time: 1590 us
  waiting for transfers between devices  1490 us (94%)
  other arithmetic  60 us (4%)
  between operations  16.1 us (1%)
    reduce_scatter x1, waiting for transfers between devices, body(): lax.psum_scatter(col_partial, 'row', scatter_dimension=1, tiled=True)  691 us
    psum x1, waiting for transfers between devices, body(): core = lax.psum(core_term, ('row', 'col')) / total_cols  469 us
    psum x1, waiting for transfers between devices, body(): gram = lax.psum(gram_term, 'row') / total_rows  252 us
    psum x1, waiting for transfers between devices, body(): sketch = lax.psum(partial_value, 'col')  81.6 us
    another operation x6, other arithmetic, orthonormalize(): factor = jnp.linalg.cholesky(gram)  34 us
  transfers between devices with their start and end apart: 4, of which 4 were waited for; matrix products, arithmetic and copies ran while one was open for 0% of the time, Pallas kernels for 0%

commit v1 on v0

v1 whole, which is shorter than its diff:
```python
import functools

import jax
import jax.numpy as jnp
from jax import lax
from jax.experimental import pallas as pl
from jax.experimental.pallas import tpu as pltpu
from jax.sharding import PartitionSpec as P

MESH = pl.DeviceIdType.MESH
HI = lax.Precision.HIGHEST
F32 = jnp.float32

RB = 8
BS = 128
RANK = 256
NY, NZ, NX, NK = 4, 16, 4, 2
NQ = NY * NX * NK
PIECE = RANK // NQ
STRIP = 48
PB = 32
FAR = (6, -6, 2, -2)


def inverse_factor(a_ref, out_ref):
    n = a_ref.shape[0]
    lane = lax.broadcasted_iota(jnp.int32, (PB, n), 1)
    sub = lax.broadcasted_iota(jnp.int32, (PB, n), 0)
    sub8 = lax.broadcasted_iota(jnp.int32, (8, 128), 0)
    lane_rest = lax.broadcasted_iota(jnp.int32, (n - PB, n), 1)
    tiles, halves = PB // 8, n // 128

    def panel(p, carry):
        top = a_ref[0:PB, :]
        cols = []
        for j in range(PB):
            wide = jnp.broadcast_to(top[:, j : j + 1], (PB, 128))
            cols.append([wide[8 * t : 8 * t + 8] for t in range(tiles)])
        strip = jnp.where(lane < PB, (lane == sub).astype(F32), top)
        w = [
            [strip[8 * t : 8 * t + 8, 128 * h : 128 * h + 128] for h in range(halves)]
            for t in range(tiles)
        ]
        for k in range(PB):
            tk, sk = divmod(k, 8)
            r = lax.rsqrt(jnp.broadcast_to(cols[k][tk][sk : sk + 1], (8, 128)))
            m = [cols[k][t] * r if t >= tk else None for t in range(tiles)]
            m[tk] = jnp.where(sub8 > sk, m[tk], 0.0)
            for j in range(k + 1, PB):
                c = jnp.broadcast_to(cols[j][tk][sk : sk + 1], (8, 128)) * r
                for t in range(tk, tiles):
                    cols[j][t] = cols[j][t] - m[t] * c
            for h in range(halves):
                u = jnp.broadcast_to(w[tk][h][sk : sk + 1], (8, 128)) * r
                for t in range(tk, tiles):
                    w[t][h] = w[t][h] - m[t] * u
                w[tk][h] = jnp.where(sub8 == sk, u, w[tk][h])
        done = jnp.concatenate([jnp.concatenate(row, axis=1) for row in w], axis=0)
        placed = pltpu.roll(done, p * PB, 1)
        out_ref[pl.ds(pl.multiple_of(p * PB, PB), PB), :] = jnp.where(
            lane < (p + 1) * PB, placed, 0.0
        )
        turned = pltpu.roll(done, n - PB, 1)
        rest = pltpu.roll(jnp.where(lane_rest < PB, 0.0, a_ref[PB:n, :]), n - PB, 1)
        step = lax.dot_general(
            turned, turned, (((0,), (0,)), ((), ())), precision=HI, preferred_element_type=F32
        )
        a_ref[0 : n - PB, :] = rest - step[0 : n - PB]
        return carry

    lax.fori_loop(0, n // PB, panel, 0)


def kernel(
    vals_ref, slot_ref, count_ref, omega_ref,
    basis_ref, proj_ref, core_ref,
    part, r1, r2, own, s_all, pick, a_all, meta,
    g_send, g_recv, z_send, z_recv, g_all,
    gram, linv, prod, strip, w1, w2s, w2r,
    send_sem, r1_sem, r2_sem, s_sem, sib_sem, a_sem, m_sem, pick_sem,
    g_sem, z_sem, ag_sem, w1_sem, w2_sem,
):
    row, col = lax.axis_index("row"), lax.axis_index("col")
    z, y = row // NY, row % NY
    x, k = col // NK, col % NK
    sib = 1 - k
    q = y * (NX * NK) + col

    def at(zz, yy, xx, kk):
        return (zz * NY + yy, xx * NK + kk)

    def plane(qq):
        return (z * NY + qq // (NX * NK), qq % (NX * NK))

    def copy(src, dst, recv_sem, device):
        return pltpu.make_async_remote_copy(
            src_ref=src, dst_ref=dst, send_sem=send_sem, recv_sem=recv_sem,
            device_id=device, device_id_type=MESH,
        )

    def loop(lo, hi, f):
        def step(i, carry):
            f(i)
            return carry

        lax.fori_loop(lo, hi, step, 0)

    barrier = pltpu.get_barrier_semaphore()

    def greet_plane(j):
        pl.semaphore_signal(
            barrier, inc=1, device_id=plane((q + j) % NQ), device_id_type=MESH
        )

    def greet_ring(j):
        pl.semaphore_signal(
            barrier, inc=1, device_id=at((z + j) % NZ, y, x, k), device_id_type=MESH
        )

    loop(1, NZ, greet_ring)
    loop(1, NQ, greet_plane)

    col_blocks = omega_ref.shape[0]
    slots = vals_ref.shape[0]
    row_of, live, prods = [], [], []
    for b in range(slots):
        slot = slot_ref[b, 0]
        on = count_ref[0, 0] > b
        row_of.append(slot // col_blocks)
        live.append(jnp.where(on, 1.0, 0.0).astype(F32))
        picked = omega_ref[pl.ds(slot % col_blocks, 1)].reshape(BS, RANK)
        prods.append(jnp.dot(vals_ref[b], picked, preferred_element_type=F32))
        a_all[pl.ds(y, 1), b] = (vals_ref[b] * live[b].astype(jnp.bfloat16))[None]
        meta[pl.ds(y, 1), b] = jnp.full(
            (1,) + meta.shape[2:], jnp.where(on, slot % col_blocks, -1), jnp.int32
        )

    def fill(kk):
        for xx in range(NX):
            block = xx * NK + kk
            total = None
            for b in range(slots):
                term = prods[b] * (jnp.where(row_of[b] == block, 1.0, 0.0).astype(F32) * live[b])
                total = term if total is None else total + term
            part[pl.ds(kk, 1), xx] = total[None]

    fill(sib)
    pl.semaphore_wait(barrier, NQ - 1 + NZ - 1)

    to_sib = at(z, y, x, sib)

    def sib_copy(xx):
        return copy(part.at[sib, xx], r1.at[xx], r1_sem.at[xx], to_sib)

    def x_copy(d):
        xx = (x + d) % NX
        return copy(part.at[k, xx], r2.at[d - 1], r2_sem.at[d - 1], at(z, y, xx, k))

    order = (2, 1, 3, 0)
    for d in order:
        sib_copy((x + d) % NX).start()
    fill(k)
    for d in order:
        xx = (x + d) % NX
        sib_copy(xx).wait_recv()
        part[pl.ds(k, 1), pl.ds(xx, 1)] = (
            part[pl.ds(k, 1), pl.ds(xx, 1)] + r1[pl.ds(xx, 1)][None]
        )
        if d:
            x_copy(d).start()

    def a_copies(d):
        to = at(z, (y + d) % NY, x, k)
        return (
            copy(a_all.at[y], a_all.at[y], a_sem.at[d - 1], to),
            copy(meta.at[y], meta.at[y], m_sem.at[d - 1], to),
        )

    for d in (2, 1, 3):
        for c in a_copies(d):
            c.start()
    for d in (1, 3, 2):
        x_copy(d).wait_recv()
    own[...] = (
        part[pl.ds(k, 1), pl.ds(x, 1)].reshape(BS, RANK) + r2[0] + r2[1] + r2[2]
    )

    def gram_of(rows):
        return lax.dot_general(
            rows, rows, (((0,), (0,)), ((), ())), precision=HI, preferred_element_type=F32
        )

    def reduce_start(u, term):
        g_send[u] = term.reshape(NQ, PIECE, RANK)

        def send(j):
            qq = (q + j) % NQ
            copy(g_send.at[u, qq], g_recv.at[u, q], g_sem.at[u, q], plane(qq)).start()

        loop(1, NQ, send)
        g_recv[u, pl.ds(q, 1)] = g_send[u, pl.ds(q, 1)]

    def reduce_plane(u):
        def arrive(j):
            qq = (q + j) % NQ
            copy(g_send.at[u, q], g_recv.at[u, qq], g_sem.at[u, qq], plane(qq)).wait_recv()

        loop(1, NQ, arrive)
        total = g_recv[u, 0]
        for i in range(1, NQ):
            total = total + g_recv[u, i]
        z_send[u] = total
        z_recv[u, pl.ds(z, 1)] = total[None]

        def send(j):
            copy(
                z_send.at[u], z_recv.at[u, z], z_sem.at[u, z], at((z + j) % NZ, y, x, k)
            ).start()

        for j in (8, 7, 9, 6, 10, 5, 11, 4, 12, 3, 13, 2, 14, 1, 15):
            send(j)

    def reduce_ring(u):
        def arrive(j):
            zz = (z + j) % NZ
            copy(z_send.at[u], z_recv.at[u, zz], z_sem.at[u, zz], at(zz, y, x, k)).wait_recv()

        loop(1, NZ, arrive)
        total = z_recv[u, 0]
        for i in range(1, NZ):
            total = total + z_recv[u, i]
        g_all[u, pl.ds(q, 1)] = total[None]

        def send(j):
            copy(g_all.at[u, q], g_all.at[u, q], ag_sem.at[u, q], plane((q + j) % NQ)).start()

        loop(1, NQ, send)

    def gather_plane(u):
        def arrive(j):
            qq = (q + j) % NQ
            copy(g_all.at[u, q], g_all.at[u, qq], ag_sem.at[u, qq], plane(qq)).wait_recv()

        loop(1, NQ, arrive)
        return g_all[u].reshape(RANK, RANK)

    reduce_start(0, gram_of(own[...]))
    reduce_plane(0)

    def s_copy(d):
        return copy(own, s_all.at[k, x], s_sem.at[d - 1], at(z, y, (x + d) % NX, k))

    def s_arrival(d):
        return copy(own, s_all.at[k, (x + NX - d) % NX], s_sem.at[d - 1], to_sib)

    s_all[pl.ds(k, 1), pl.ds(x, 1)] = own[...][None, None]
    for d in (2, 1, 3):
        s_copy(d).start()
    reduce_ring(0)
    for d in (1, 3, 2):
        s_arrival(d).wait_recv()
    s_sib = copy(s_all.at[k], s_all.at[k], sib_sem, to_sib)
    s_sib.start()
    copy(s_all.at[k], s_all.at[sib], sib_sem, to_sib).wait_recv()
    for b in range(slots):
        rows = s_all[pl.ds(row_of[b] % NK, 1), pl.ds(row_of[b] // NK, 1)]
        pick[pl.ds(y, 1), b] = rows.reshape(1, BS, RANK)
    gram[...] = gather_plane(0) * (1.0 / (BS * RB * NY * NZ))

    def pick_copy(d):
        return copy(pick.at[y], pick.at[y], pick_sem.at[d - 1], at(z, (y + d) % NY, x, k))

    def pick_arrival(d):
        yy = (y + NY - d) % NY
        return copy(pick.at[y], pick.at[yy], pick_sem.at[d - 1], at(z, yy, x, k))

    for d in (2, 1, 3):
        pick_copy(d).start()
    inverse_factor(gram, linv)

    def basis_rows(rows):
        return lax.dot_general(
            rows, linv[...], (((1,), (1,)), ((), ())), precision=HI, preferred_element_type=F32
        ).astype(jnp.bfloat16)

    basis_ref[...] = basis_rows(own[...])

    def products(yy):
        for b in range(slots):
            rows = basis_rows(pick[pl.ds(yy, 1), b].reshape(BS, RANK))
            block = a_all[pl.ds(yy, 1), b].reshape(BS, BS)
            prod[pl.ds(yy, 1), b] = lax.dot_general(
                block, rows, (((0,), (0,)), ((), ())), preferred_element_type=F32
            )[None]

    products(y)
    for d in (1, 3, 2):
        yy = (y + NY - d) % NY
        to = at(z, yy, x, k)
        copy(a_all.at[y], a_all.at[yy], a_sem.at[d - 1], to).wait_recv()
        copy(meta.at[y], meta.at[yy], m_sem.at[d - 1], to).wait_recv()
        pick_arrival(d).wait_recv()
        products(yy)

    tile = 16
    per_strip = STRIP // tile

    def place(zz):
        for t in range(per_strip):
            g = zz * (NY * per_strip) + y * per_strip + t
            block, rows = g // (BS // tile), pl.multiple_of(g % (BS // tile) * tile, tile)
            total = jnp.zeros((tile, RANK), F32)
            for yy in range(NY):
                for b in range(slots):
                    total = total + jnp.where(
                        meta[yy, b] == block, prod[yy, b, pl.ds(rows, tile), :], 0.0
                    )
            strip[pl.ds(zz, 1), pl.ds(t * tile, tile), :] = total[None]

    loop(0, NZ, place)

    sign = 1 - 2 * k
    near = (1, -1, 2)

    def w1_copy(i, e):
        mid = (z + sign * near[i] + NZ) % NZ
        dest = (mid + FAR[e] + NZ) % NZ
        return copy(strip.at[dest], w1.at[e, i], w1_sem.at[e, i], at(mid, y, x, k))

    def w2_copy(e):
        return copy(w2s.at[e], w2r.at[e], w2_sem.at[e], at((z + FAR[e] + NZ) % NZ, y, x, k))

    for e in range(4):
        for i in (2, 0, 1):
            w1_copy(i, e).start()
    for e in range(4):
        for i in range(3):
            w1_copy(i, e).wait_recv()
        dest = (z + FAR[e] + NZ) % NZ
        mine = strip[pl.ds(dest, 1)].reshape(STRIP, RANK)
        w2s[e] = mine + w1[e, 0] + w1[e, 1] + w1[e, 2]
        w2_copy(e).start()
    for e in (2, 3, 0, 1):
        w2_copy(e).wait_recv()
    proj = (w2r[0] + w2r[1] + w2r[2] + w2r[3]) * (1.0 / 256.0)
    proj_ref[0] = proj

    reduce_start(1, gram_of(proj))
    reduce_plane(1)
    reduce_ring(1)
    core_ref[...] = gather_plane(1) / float(col_blocks * BS * NX * NK)

    for xx in range(NX):
        sib_copy(xx).wait_send()
    for d in (1, 2, 3):
        x_copy(d).wait_send()
        s_copy(d).wait_send()
        pick_copy(d).wait_send()
        for c in a_copies(d):
            c.wait_send()
    s_sib.wait_send()
    for u in range(2):

        def sent_plane(j):
            copy(g_send.at[u, q], g_recv.at[u, q], g_sem.at[u, q], to_sib).wait_send()
            copy(g_all.at[u, q], g_all.at[u, q], ag_sem.at[u, q], to_sib).wait_send()

        def sent_ring(j):
            copy(z_send.at[u], z_recv.at[u, z], z_sem.at[u, z], to_sib).wait_send()

        loop(1, NQ, sent_plane)
        loop(1, NZ, sent_ring)
    for e in range(4):
        for i in range(3):
            w1_copy(i, e).wait_send()
        w2_copy(e).wait_send()


def body(block_vals, block_slot, block_count, omega):
    slots = block_vals.shape[0]
    vmem, smem = pl.BlockSpec(memory_space=pltpu.VMEM), pl.BlockSpec(memory_space=pltpu.SMEM)
    dma = pltpu.SemaphoreType.DMA
    blocks = lambda *lead: pltpu.VMEM((*lead, BS, RANK), F32)
    basis, projected, core = pl.pallas_call(
        kernel,
        out_shape=(
            jax.ShapeDtypeStruct((BS, RANK), jnp.bfloat16),
            jax.ShapeDtypeStruct((1, STRIP, RANK), F32),
            jax.ShapeDtypeStruct((RANK, RANK), F32),
        ),
        in_specs=[vmem, smem, smem, vmem],
        out_specs=(vmem, vmem, vmem),
        scratch_shapes=[
            blocks(NK, NX),
            blocks(NX),
            blocks(NX - 1),
            blocks(),
            blocks(NK, NX),
            blocks(NY, slots),
            pltpu.VMEM((NY, slots, BS, BS), jnp.bfloat16),
            pltpu.VMEM((NY, slots, 16, RANK), jnp.int32),
            pltpu.VMEM((2, NQ, PIECE, RANK), F32),
            pltpu.VMEM((2, NQ, PIECE, RANK), F32),
            pltpu.VMEM((2, PIECE, RANK), F32),
            pltpu.VMEM((2, NZ, PIECE, RANK), F32),
            pltpu.VMEM((2, NQ, PIECE, RANK), F32),
            pltpu.VMEM((RANK, RANK), F32),
            pltpu.VMEM((RANK, RANK), F32),
            blocks(NY, slots),
            pltpu.VMEM((NZ, STRIP, RANK), F32),
            pltpu.VMEM((4, 3, STRIP, RANK), F32),
            pltpu.VMEM((4, STRIP, RANK), F32),
            pltpu.VMEM((4, STRIP, RANK), F32),
            dma,
            dma((NX,)), dma((NX - 1,)), dma((NX - 1,)), dma, dma((NY - 1,)), dma((NY - 1,)), dma((NY - 1,)),
            dma((2, NQ)), dma((2, NZ)), dma((2, NQ)), dma((4, 3)), dma((4,)),
        ],
        compiler_params=pltpu.CompilerParams(
            collective_id=0, has_side_effects=True, vmem_limit_bytes=48 * 2**20
        ),
        name="range_basis",
    )(block_vals, block_slot, block_count, omega.reshape(-1, BS, RANK))
    return basis, projected, core


def solution(mesh):
    placed = (P("row", "col", None), P("row", "col"), P("row", "col"), P("col", None))
    return jax.shard_map(
        body,
        mesh=mesh,
        in_specs=placed,
        out_specs=(P(("row", "col"), None), P("col", "row", None), P()),
        check_vma=False,
    )
```

time: 1590 us -> 117 us (0.07)
  waiting for transfers between devices: 1490 us -> 0 us
  Pallas kernels: 0 us -> 111 us
  other arithmetic: 60 us -> 0 us
    psum x3 -> x0, waiting for transfers between devices: 803 us -> none  [the longest x1 469 us: body(): core = lax.psum(core_term, ('row', 'col')) / total_cols]
    reduce_scatter x1 -> x0, waiting for transfers between devices: 691 us -> none  [body(): lax.psum_scatter(col_partial, 'row', scatter_dimension=1, tiled=True)]
    pallas_call x0 -> x1, Pallas kernels: none -> 111 us  [body(): pl.pallas_call(kernel, out_shape=(jax.ShapeDtypeStruct((BS, RANK), jnp.bf...]
    another operation x9 -> x0, other arithmetic: 54.2 us -> none  [the longest x6 34 us: orthonormalize(): factor = jnp.linalg.cholesky(gram)]
  transfers between devices with their start and end apart: 4 -> 0, of which waited for: 4 -> 0; matrix products, arithmetic and copies ran while one was open for 0% -> 0% of each run, Pallas kernels for 0% -> 0%
where the time goes in v1:
time: 117 us
  Pallas kernels  111 us (95%)
  local copies, waits for them, and re-layouts  4.94 us (4%)
  between operations  1.29 us (1%)
    pallas_call x1, Pallas kernels, body(): pl.pallas_call(kernel, out_shape=(jax.ShapeDtypeStruct((BS, RANK), jnp.bf...  111 us
    unnamed x8, local copies, waits for them, and re-layouts  4.94 us

profile of v1, /device:TPU:1, one launch (start us, length us, event | category | flops | bytes accessed | tf_op | source)
XLA Modules:
  0.0 117.0 jit_solution(132918555192360467)
XLA Ops:
  1.3 0.7 copy.7.slot_ref
  2.0 0.0 copy-start
  2.0 1.4 %copy-done = bf16[3072,256]{1,0:T(8,128)(2,1)S(1)} copy-done((bf16[3072,256]{1,0:T(8,128)(2,1)S(1)}, bf16[3072,256]{1,0:T(8,128)(2,1)}, u32[]{:S(2)}) %copy-start) | copy-done | bytes 1572888
  3.4 0.0 copy-start.1
  3.4 0.8 copy-done.1
  4.3 110.8 %range_basis.1 = (bf16[128,256]{1,0:T(8,128)(2,1)S(1)}, f32[1,48,256]{2,1,0:T(8,128)S(1)}, f32[256,256]{1,0:T(8,128)S(1)}) custom-call(bf16[2,128,128]{2,1,0:T(8,128)(2,1)S(1)} %copy-done.1, s32[2,1]{1,0:T(2,128)S(1)} %copy.7.slot_ref, s32[1,1]{1,0:T(1,128)S(6)} %copy.11.count_ref, bf16[24,128,256]{2,1,0:T(8,128)(2,1)S(1)} %bitcast.1), custom_call_target="tpu_custom_call" | custom-call | tf_op jit(solution)/shard_map/range_basis/pallas_call | solution.py:384
  115.1 0.6 copy.12
  115.7 0.6 copy.13
  116.3 0.7 copy.14
Async XLA Ops:
  2.0 1.4 %copy-start = (bf16[3072,256]{1,0:T(8,128)(2,1)S(1)}, bf16[3072,256]{1,0:T(8,128)(2,1)}, u32[]{:S(2)}) copy-start(bf16[3072,256]{1,0:T(8,128)(2,1)} %param.7) | copy-start | bytes 4718596
  3.4 0.8 copy-start.1

commit v2 on v1

v2 whole, which is shorter than its diff:
```python
import functools

import jax
import jax.numpy as jnp
from jax import lax
from jax.experimental import pallas as pl
from jax.experimental.pallas import tpu as pltpu
from jax.sharding import PartitionSpec as P

MESH = pl.DeviceIdType.MESH
HI = lax.Precision.HIGHEST
F32 = jnp.float32

RB = 8
BS = 128
RANK = 256
NY, NZ, NX, NK = 4, 16, 4, 2
NQ = NY * NX
HALF = RANK // NK
PIECE = HALF // NQ
STRIP = 48
PB, SB = 64, 16
NG = 4
STEPS = 32767.0
FAR = (6, -6, 2, -2)


def inverse_factor(a_ref, out_ref):
    n = a_ref.shape[0]
    lane = lax.broadcasted_iota(jnp.int32, (PB, n), 1)
    lane8 = lax.broadcasted_iota(jnp.int32, (8, 128), 1)
    sub8 = lax.broadcasted_iota(jnp.int32, (8, 128), 0)
    lane_rest = lax.broadcasted_iota(jnp.int32, (n - PB, n), 1)
    tiles, halves = PB // 8, n // 128

    def wide(v, i):
        return jnp.broadcast_to(v[i : i + 1], (8, 128))

    def panel(p, carry):
        w = [
            [a_ref[8 * t : 8 * t + 8, 128 * h : 128 * h + 128] for h in range(halves)]
            for t in range(tiles)
        ]
        for base in range(0, PB, SB):
            first, last = base // 8, (base + SB) // 8
            cols = [
                {
                    t: jnp.broadcast_to(w[t][0][:, base + j : base + j + 1], (8, 128))
                    for t in range(first, tiles)
                }
                for j in range(SB)
            ]
            inside = (lane8 >= base) & (lane8 < base + SB)
            for t in range(tiles):
                fresh = jnp.where(lane8 == sub8 + 8 * t, 1.0, 0.0) if first <= t < last else 0.0
                w[t][0] = jnp.where(inside, fresh, w[t][0])
            for k in range(SB):
                tk, sk = divmod(base + k, 8)
                r = lax.rsqrt(wide(cols[k][tk], sk))
                m = {t: cols[k][t] * r for t in range(tk, tiles)}
                m[tk] = jnp.where(sub8 > sk, m[tk], 0.0)
                for j in range(k + 1, SB):
                    c = wide(cols[j][tk], sk) * r
                    for t in range(tk, tiles):
                        cols[j][t] = cols[j][t] - m[t] * c
                for h in range(halves):
                    u = wide(w[tk][h], sk) * r
                    for t in range(tk, tiles):
                        w[t][h] = w[t][h] - m[t] * u
                    w[tk][h] = jnp.where(sub8 == sk, u, w[tk][h])
        done = jnp.concatenate([jnp.concatenate(r, axis=1) for r in w], axis=0)
        placed = pltpu.roll(done, p * PB, 1)
        out_ref[pl.ds(pl.multiple_of(p * PB, PB), PB), :] = jnp.where(
            lane < (p + 1) * PB, placed, 0.0
        )
        turned = pltpu.roll(done, n - PB, 1)
        rest = pltpu.roll(jnp.where(lane_rest < PB, 0.0, a_ref[PB:n, :]), n - PB, 1)
        step = lax.dot_general(
            turned, turned, (((0,), (0,)), ((), ())), precision=HI, preferred_element_type=F32
        )
        a_ref[0 : n - PB, :] = rest - step[0 : n - PB]
        return carry

    lax.fori_loop(0, n // PB, panel, 0)


def kernel(
    vals_hbm, slot_hbm, omega_hbm, count_ref,
    basis_ref, proj_ref, core_ref,
    vals_ref, slot_ref, omega_ref,
    part, r1, r2, own, s_all, pick, ready, a_all, meta,
    pair, g_send, g_recv, z_near, z_far, g_all,
    gram, linv, prod, strip, code1, unit1, code2, unit2, w1, c1, w2, c2,
    load_sem, send_sem, r1_sem, r2_sem, s_sem, sib_sem, a_sem, m_sem, pick_sem, ready_sem,
    pair_sem, g_sem, near_sem, far_sem, ag_sem, half_sem, w1_sem, c1_sem, w2_sem, c2_sem,
):
    row, col = lax.axis_index("row"), lax.axis_index("col")
    z, y = row // NY, row % NY
    x, k = col // NK, col % NK
    sib = 1 - k
    q = y * NX + x
    pending = []

    def at(zz, yy, xx, kk):
        return (zz * NY + yy, xx * NK + kk)

    def plane(qq):
        return at(z, qq // NX, qq % NX, k)

    to_sib = at(z, y, x, sib)

    def copy(src, dst, recv_sem, device):
        return pltpu.make_async_remote_copy(
            src_ref=src, dst_ref=dst, send_sem=send_sem, recv_sem=recv_sem,
            device_id=device, device_id_type=MESH,
        )

    def go(c):
        c.start()
        pending.append(c.wait_send)

    barrier = pltpu.get_barrier_semaphore()

    def greet(device):
        pl.semaphore_signal(barrier, inc=1, device_id=device, device_id_type=MESH)

    reach = (6, -6, 5, -5, 4, -4, 3, -3, 2, -2, 1, -1)
    for j in reach:
        greet(at((z + j + NZ) % NZ, y, x, k))
    for j in range(1, NQ):
        greet(plane((q + j) % NQ))
    greet(to_sib)

    pairs = ((slot_hbm, slot_ref), (vals_hbm, vals_ref), (omega_hbm, omega_ref))
    loads = [pltpu.make_async_copy(a, b, load_sem.at[i]) for i, (a, b) in enumerate(pairs)]
    for load in loads:
        load.start()
    for load in loads:
        load.wait()

    col_blocks = omega_ref.shape[0]
    slots = vals_ref.shape[0]
    row_of, live, prods = [], [], []
    for b in range(slots):
        slot = slot_ref[0, b]
        on = count_ref[0, 0] > b
        row_of.append(slot // col_blocks)
        live.append(jnp.where(on, 1.0, 0.0).astype(F32))
        picked = omega_ref[pl.ds(slot % col_blocks, 1)].reshape(BS, RANK)
        prods.append(jnp.dot(vals_ref[b], picked, preferred_element_type=F32))
        a_all[pl.ds(y, 1), b] = (vals_ref[b] * live[b].astype(jnp.bfloat16))[None]
        meta[pl.ds(y, 1), b] = jnp.full(
            (1,) + meta.shape[2:], jnp.where(on, slot % col_blocks, -1), jnp.int32
        )

    def fill(kk):
        for xx in range(NX):
            block = xx * NK + kk
            total = None
            for b in range(slots):
                term = prods[b] * (jnp.where(row_of[b] == block, 1.0, 0.0).astype(F32) * live[b])
                total = term if total is None else total + term
            part[pl.ds(kk, 1), xx] = total[None]

    fill(sib)
    pl.semaphore_wait(barrier, NQ + len(reach))

    def sib_copy(xx):
        return copy(part.at[sib, xx], r1.at[xx], r1_sem.at[xx], to_sib)

    def x_copy(d):
        xx = (x + d) % NX
        return copy(part.at[k, xx], r2.at[d - 1], r2_sem.at[d - 1], at(z, y, xx, k))

    order = (2, 1, 3, 0)
    for d in order:
        go(sib_copy((x + d) % NX))
    fill(k)
    for d in order:
        xx = (x + d) % NX
        sib_copy(xx).wait_recv()
        part[pl.ds(k, 1), pl.ds(xx, 1)] = (
            part[pl.ds(k, 1), pl.ds(xx, 1)] + r1[pl.ds(xx, 1)][None]
        )
        if d:
            go(x_copy(d))

    def a_copies(d):
        to = at(z, (y + d) % NY, x, k)
        return (
            copy(a_all.at[y], a_all.at[y], a_sem.at[d - 1], to),
            copy(meta.at[y], meta.at[y], m_sem.at[d - 1], to),
        )

    for d in (2, 1, 3):
        for c in a_copies(d):
            go(c)
    for d in (1, 3, 2):
        x_copy(d).wait_recv()
    own[...] = (
        part[pl.ds(k, 1), pl.ds(x, 1)].reshape(BS, RANK) + r2[0] + r2[1] + r2[2]
    )

    def gram_half(u, rows):
        n = rows.shape[0]
        pair[u, pl.ds(k, 1), 0:n] = rows[None]
        mine = pair.at[u, k, pl.ds(0, n)]
        swap = copy(mine, mine, pair_sem.at[u], to_sib)
        go(swap)
        copy(mine, pair.at[u, sib, pl.ds(0, n)], pair_sem.at[u], to_sib).wait_recv()
        lanes = pl.ds(pl.multiple_of(k * HALF, HALF), HALF)
        term = None
        for kk in range(NK):
            one = lax.dot_general(
                pair[u, kk, pl.ds(0, n), lanes], pair[u, kk, 0:n], (((0,), (0,)), ((), ())),
                precision=HI, preferred_element_type=F32,
            )
            term = one if term is None else term + one
        g_send[u] = term.reshape(NQ, PIECE, RANK)
        for j in range(1, NQ):
            qq = (q + j) % NQ
            go(copy(g_send.at[u, qq], g_recv.at[u, q], g_sem.at[u], plane(qq)))
        g_recv[u, pl.ds(q, 1)] = g_send[u, pl.ds(q, 1)]

    def arrived(buffer, sem):
        copy(buffer, buffer, sem, to_sib).wait_recv()

    group, member = z // NG, z % NG
    way, reach0 = member // 2 * 2 - 1, 4 - member * (3 - member)

    def reduce_plane(u):
        arrived(g_recv.at[u, pl.ds(0, NQ - 1)], g_sem.at[u])
        total = g_recv[u, 0]
        for i in range(1, NQ):
            total = total + g_recv[u, i]
        z_near[u, pl.ds(member, 1)] = total[None]
        mine = z_near.at[u, member]
        for j in range(1, NG):
            near = group * NG + (member + j) % NG
            go(copy(mine, mine, near_sem.at[u], at(near, y, x, k)))

    def reduce_near(u):
        arrived(z_near.at[u, pl.ds(0, NG - 1)], near_sem.at[u])
        total = z_near[u, 0]
        for i in range(1, NG):
            total = total + z_near[u, i]
        z_far[u, pl.ds(group, 1)] = total[None]
        mine = z_far.at[u, group]
        for j in (2, 1, 0):
            far = (z + way * (reach0 + j) + NZ) % NZ
            go(copy(mine, mine, far_sem.at[u], at(far, y, x, k)))

    def reduce_far(u):
        arrived(z_far.at[u, pl.ds(0, NZ // NG - 1)], far_sem.at[u])
        total = z_far[u, 0]
        for i in range(1, NZ // NG):
            total = total + z_far[u, i]
        g_all[u, pl.ds(k, 1), pl.ds(q, 1)] = total[None, None]
        mine = g_all.at[u, k, q]
        for j in range(1, NQ):
            go(copy(mine, mine, ag_sem.at[u], plane((q + j) % NQ)))

    def gather_plane(u):
        arrived(g_all.at[u, k, pl.ds(0, NQ - 1)], ag_sem.at[u])
        go(copy(g_all.at[u, k], g_all.at[u, k], half_sem.at[u], to_sib))
        copy(g_all.at[u, k], g_all.at[u, sib], half_sem.at[u], to_sib).wait_recv()
        return g_all[u].reshape(RANK, RANK)

    gram_half(0, own[...])

    parts = 2
    depth = BS // parts

    def s_copy(d, i):
        rows = pl.ds(i * depth, depth)
        return copy(
            own.at[rows], s_all.at[k, x, rows], s_sem.at[d - 1, i], at(z, y, (x + d) % NX, k)
        )

    def s_arrival(d, i):
        rows = pl.ds(i * depth, depth)
        return copy(
            own.at[rows], s_all.at[k, (x + NX - d) % NX, rows], s_sem.at[d - 1, i], to_sib
        )

    def pick_copy(d):
        return copy(pick.at[y], pick.at[y], pick_sem.at[d - 1], at(z, (y + d) % NY, x, k))

    def pick_arrival(d):
        yy = (y + NY - d) % NY
        return copy(pick.at[y], pick.at[yy], pick_sem.at[d - 1], at(z, yy, x, k))

    s_all[pl.ds(k, 1), pl.ds(x, 1)] = own[...][None, None]
    reduce_plane(0)
    for d in (2, 1, 3):
        go(s_copy(d, 0))
    reduce_near(0)
    for d in (2, 1, 3):
        go(s_copy(d, 1))
    reduce_far(0)
    for d in (1, 3, 2):
        for i in range(parts):
            s_arrival(d, i).wait_recv()
    go(copy(s_all.at[k], s_all.at[k], sib_sem, to_sib))
    copy(s_all.at[k], s_all.at[sib], sib_sem, to_sib).wait_recv()
    for b in range(slots):
        rows = s_all[pl.ds(row_of[b] % NK, 1), pl.ds(row_of[b] // NK, 1)]
        pick[pl.ds(y, 1), b] = rows.reshape(1, BS, RANK)
    gram[...] = gather_plane(0) * (1.0 / (BS * RB * NY * NZ))

    for d in (1, 3):
        go(pick_copy(d))
    inverse_factor(gram, linv)

    def basis_rows(rows):
        return lax.dot_general(
            rows, linv[...], (((1,), (1,)), ((), ())), precision=HI, preferred_element_type=F32
        ).astype(jnp.bfloat16)

    across = (y + 2) % NY
    for b in range(slots):
        ready[pl.ds(y, 1), b] = basis_rows(pick[pl.ds(y, 1), b].reshape(BS, RANK))[None]
    go(copy(ready.at[y], ready.at[y], ready_sem, at(z, across, x, k)))
    basis_ref[...] = basis_rows(own[...])

    def products(yy, formed):
        for b in range(slots):
            if formed:
                rows = ready[pl.ds(yy, 1), b].reshape(BS, RANK)
            else:
                rows = basis_rows(pick[pl.ds(yy, 1), b].reshape(BS, RANK))
            block = a_all[pl.ds(yy, 1), b].reshape(BS, BS)
            prod[pl.ds(yy, 1), b] = lax.dot_general(
                block, rows, (((0,), (0,)), ((), ())), preferred_element_type=F32
            )[None]

    products(y, True)
    for d in (1, 3, 2):
        yy = (y + NY - d) % NY
        to = at(z, yy, x, k)
        copy(a_all.at[y], a_all.at[yy], a_sem.at[d - 1], to).wait_recv()
        copy(meta.at[y], meta.at[yy], m_sem.at[d - 1], to).wait_recv()
        if d == 2:
            copy(ready.at[y], ready.at[yy], ready_sem, to).wait_recv()
        else:
            pick_arrival(d).wait_recv()
        products(yy, d == 2)

    tile = 16
    per_strip = STRIP // tile

    def coded(v):
        top = jnp.maximum(jnp.max(jnp.abs(v), axis=0, keepdims=True), 1e-33)
        return jnp.round(v * (STEPS / top)).astype(jnp.int32).astype(jnp.int16), top * (1.0 / STEPS)

    def value(steps, unit):
        return steps.astype(jnp.int32).astype(F32) * unit

    def place(zz, carry):
        totals = []
        for t in range(per_strip):
            g = zz * (NY * per_strip) + y * per_strip + t
            block, rows = g // (BS // tile), pl.multiple_of(g % (BS // tile) * tile, tile)
            total = jnp.zeros((tile, RANK), F32)
            for yy in range(NY):
                for b in range(slots):
                    here = jnp.concatenate([meta[yy, b] == block] * (RANK // 128), axis=1)
                    total = total + jnp.where(here, prod[yy, b, pl.ds(rows, tile), :], 0.0)
            totals.append(total)
        total = jnp.concatenate(totals, axis=0)
        strip[pl.ds(zz, 1)] = total[None]
        steps, unit = coded(total)
        code1[pl.ds(zz, 1)] = steps[None]
        unit1[pl.ds(zz, 1), :] = unit
        return carry

    lax.fori_loop(0, NZ, place, 0)

    sign = 1 - 2 * k
    near = (1, -1, 2)

    def w1_copy(i, e):
        mid = (z + sign * near[i] + NZ) % NZ
        dest = (mid + FAR[e] + NZ) % NZ
        return copy(code1.at[dest], w1.at[e, i], w1_sem.at[e, i], at(mid, y, x, k))

    def c1_copy(i):
        return copy(unit1, c1.at[i], c1_sem.at[i], at((z + sign * near[i] + NZ) % NZ, y, x, k))

    def w2_copies(e):
        to = at((z + FAR[e] + NZ) % NZ, y, x, k)
        return (
            copy(code2.at[e], w2.at[e], w2_sem.at[e], to),
            copy(unit2.at[e], c2.at[e], c2_sem.at[e], to),
        )

    for i in (2, 0, 1):
        go(c1_copy(i))
    for e in range(4):
        for i in (2, 0, 1):
            go(w1_copy(i, e))
    for i in range(3):
        c1_copy(i).wait_recv()
    for e in range(4):
        for i in range(3):
            w1_copy(i, e).wait_recv()
        dest = (z + FAR[e] + NZ) % NZ
        total = strip[pl.ds(dest, 1)].reshape(STRIP, RANK)
        for i in range(3):
            total = total + value(w1[e, i], c1[i, pl.ds(dest, 1), :])
        code2[e], unit2[e] = coded(total)
        for c in w2_copies(e):
            go(c)
    proj = jnp.zeros((STRIP, RANK), F32)
    for e in range(4):
        for c in w2_copies(e):
            c.wait_recv()
        proj = proj + value(w2[e], c2[e])
    proj = proj * (1.0 / 256.0)
    proj_ref[0] = proj

    gram_half(1, proj)
    reduce_plane(1)
    reduce_near(1)
    reduce_far(1)
    core_ref[...] = gather_plane(1) / float(col_blocks * BS * NX * NK)

    for wait in pending:
        wait()


def body(block_vals, block_slot, block_count, omega):
    slots = block_vals.shape[0]
    vmem = pl.BlockSpec(memory_space=pltpu.VMEM)
    hbm = pl.BlockSpec(memory_space=pltpu.HBM)
    dma = pltpu.SemaphoreType.DMA
    blocks = lambda *lead: pltpu.VMEM((*lead, BS, RANK), F32)
    inputs = [
        pltpu.with_memory_space_constraint(a, pltpu.HBM)
        for a in (block_vals, block_slot.T, omega.reshape(-1, BS, RANK))
    ]
    basis, projected, core = pl.pallas_call(
        kernel,
        out_shape=(
            pltpu.VMEM((BS, RANK), jnp.bfloat16),
            pltpu.VMEM((1, STRIP, RANK), F32),
            pltpu.VMEM((RANK, RANK), F32),
        ),
        in_specs=[hbm] * 3 + [pl.BlockSpec(memory_space=pltpu.SMEM)],
        out_specs=(vmem, vmem, vmem),
        scratch_shapes=[
            pltpu.VMEM(block_vals.shape, block_vals.dtype),
            pltpu.SMEM(block_slot.shape[::-1], jnp.int32),
            pltpu.VMEM((omega.shape[0] // BS, BS, RANK), omega.dtype),
            blocks(NK, NX),
            blocks(NX),
            blocks(NX - 1),
            blocks(),
            blocks(NK, NX),
            blocks(NY, slots),
            pltpu.VMEM((NY, slots, BS, RANK), jnp.bfloat16),
            pltpu.VMEM((NY, slots, BS, BS), jnp.bfloat16),
            pltpu.VMEM((NY, slots, 16, 128), jnp.int32),
            blocks(2, NK),
            pltpu.VMEM((2, NQ, PIECE, RANK), F32),
            pltpu.VMEM((2, NQ, PIECE, RANK), F32),
            pltpu.VMEM((2, NG, PIECE, RANK), F32),
            pltpu.VMEM((2, NZ // NG, PIECE, RANK), F32),
            pltpu.VMEM((2, NK, NQ, PIECE, RANK), F32),
            pltpu.VMEM((RANK, RANK), F32),
            pltpu.VMEM((RANK, RANK), F32),
            blocks(NY, slots),
            pltpu.VMEM((NZ, STRIP, RANK), F32),
            pltpu.VMEM((NZ, STRIP, RANK), jnp.int16),
            pltpu.VMEM((NZ, RANK), F32),
            pltpu.VMEM((4, STRIP, RANK), jnp.int16),
            pltpu.VMEM((4, 1, RANK), F32),
            pltpu.VMEM((4, 3, STRIP, RANK), jnp.int16),
            pltpu.VMEM((3, NZ, RANK), F32),
            pltpu.VMEM((4, STRIP, RANK), jnp.int16),
            pltpu.VMEM((4, 1, RANK), F32),
            dma((3,)), dma,
            dma((NX,)), dma((NX - 1,)), dma((NX - 1, 2)), dma, dma((NY - 1,)), dma((NY - 1,)), dma((NY - 1,)), dma,
            dma((2,)), dma((2,)), dma((2,)), dma((2,)), dma((2,)), dma((2,)), dma((4, 3)), dma((3,)), dma((4,)), dma((4,)),
        ],
        compiler_params=pltpu.CompilerParams(
            collective_id=0, has_side_effects=True, vmem_limit_bytes=60 * 2**20
        ),
        name="range_basis",
    )(*inputs, block_count)
    return basis, projected, core


def solution(mesh):
    placed = (P("row", "col", None), P("row", "col"), P("row", "col"), P("col", None))
    return jax.shard_map(
        body,
        mesh=mesh,
        in_specs=placed,
        out_specs=(P(("row", "col"), None), P("col", "row", None), P()),
        check_vma=False,
    )
```

time: 117 us -> 103 us (0.88)
  Pallas kernels: 111 us -> 99.4 us
  local copies, waits for them, and re-layouts: 4.94 us -> 1.95 us
    pallas_call x1, Pallas kernels: 111 us -> 99.4 us  [body(): pl.pallas_call(kernel, out_shape=(pltpu.VMEM((BS, RANK), jnp.bfloat16), p...]
    unnamed x8 -> x3, local copies, waits for them, and re-layouts: 4.94 us -> 1.95 us
where the time goes in v2:
time: 103 us
  Pallas kernels  99.4 us (97%)
  local copies, waits for them, and re-layouts  1.95 us (2%)
  between operations  1.29 us (1%)
    pallas_call x1, Pallas kernels, body(): pl.pallas_call(kernel, out_shape=(pltpu.VMEM((BS, RANK), jnp.bfloat16), p...  99.4 us

profile of v2, /device:TPU:1, one launch (start us, length us, event | category | flops | bytes accessed | tf_op | source)
XLA Modules:
  0.0 102.6 jit_solution(17169957517263982962)
XLA Ops:
  1.3 99.4 %range_basis.1 = (bf16[128,256]{1,0:T(8,128)(2,1)S(1)}, f32[1,48,256]{2,1,0:T(8,128)S(1)}, f32[256,256]{1,0:T(8,128)S(1)}) custom-call(bf16[2,128,128]{2,1,0:T(8,128)(2,1)} %vals_hbm.1, s32[1,2]{1,0:T(1,128)} %bitcast.3, bf16[24,128,256]{2,1,0:T(8,128)(2,1)} %bitcast.2, s32[1,1]{1,0:T(1,128)S(6)} %copy.13.count_ref), custom_call_target="tpu_custom_call" | custom-call | tf_op jit(solution)/shard_map/range_basis/pallas_call | solution.py:442
  100.7 0.6 copy.10
  101.3 0.6 copy.11
  101.9 0.7 copy.12

commit v3 on v2

--- a/solution.py
+++ b/solution.py
@@ -73,12 +73,16 @@
         out_ref[pl.ds(pl.multiple_of(p * PB, PB), PB), :] = jnp.where(
             lane < (p + 1) * PB, placed, 0.0
         )
-        turned = pltpu.roll(done, n - PB, 1)
-        rest = pltpu.roll(jnp.where(lane_rest < PB, 0.0, a_ref[PB:n, :]), n - PB, 1)
-        step = lax.dot_general(
-            turned, turned, (((0,), (0,)), ((), ())), precision=HI, preferred_element_type=F32
-        )
-        a_ref[0 : n - PB, :] = rest - step[0 : n - PB]
+
+        @pl.when(p < n // PB - 1)
+        def _():
+            turned = pltpu.roll(done, n - PB, 1)
+            rest = pltpu.roll(jnp.where(lane_rest < PB, 0.0, a_ref[PB:n, :]), n - PB, 1)
+            step = lax.dot_general(
+                turned, turned, (((0,), (0,)), ((), ())), precision=HI, preferred_element_type=F32
+            )
+            a_ref[0 : n - PB, :] = rest - step[0 : n - PB]
+
         return carry
 
     lax.fori_loop(0, n // PB, panel, 0)
@@ -88,24 +92,28 @@
     vals_hbm, slot_hbm, omega_hbm, count_ref,
     basis_ref, proj_ref, core_ref,
     vals_ref, slot_ref, omega_ref,
-    part, r1, r2, own, s_all, pick, ready, a_all, meta,
-    pair, g_send, g_recv, z_near, z_far, g_all,
+    part, r1, relay, r2, own, s_all, pick, ready, a_all, meta,
+    pair0, pair1, g_send, g_recv, z_near, z_far, g_all,
     gram, linv, prod, strip, code1, unit1, code2, unit2, w1, c1, w2, c2,
-    load_sem, send_sem, r1_sem, r2_sem, s_sem, sib_sem, a_sem, m_sem, pick_sem, ready_sem,
+    beyond_sem, load_sem, send_sem, r1_sem, relay_sem, r2_sem, s_sem, sib_sem, a_sem, m_sem, pick_sem, ready_sem,
     pair_sem, g_sem, near_sem, far_sem, ag_sem, half_sem, w1_sem, c1_sem, w2_sem, c2_sem,
 ):
     row, col = lax.axis_index("row"), lax.axis_index("col")
-    z, y = row // NY, row % NY
-    x, k = col // NK, col % NK
+    z, y = lax.div(row, NY), lax.rem(row, NY)
+    x, k = lax.div(col, NK), lax.rem(col, NK)
     sib = 1 - k
     q = y * NX + x
     pending = []
+    pairs = (pair0, pair1)
+
+    def around(i, n):
+        return lax.rem(i + n, n)
 
     def at(zz, yy, xx, kk):
         return (zz * NY + yy, xx * NK + kk)
 
     def plane(qq):
-        return at(z, qq // NX, qq % NX, k)
+        return at(z, lax.div(qq, NX), lax.rem(qq, NX), k)
 
     to_sib = at(z, y, x, sib)
 
@@ -119,22 +127,27 @@
         c.start()
         pending.append(c.wait_send)
 
+    def flush():
+        while pending:
+            pending.pop(0)()
+
+    moves = ((slot_hbm, slot_ref), (vals_hbm, vals_ref), (omega_hbm, omega_ref))
+    loads = [pltpu.make_async_copy(a, b, load_sem.at[i]) for i, (a, b) in enumerate(moves)]
+    for load in loads:
+        load.start()
+
     barrier = pltpu.get_barrier_semaphore()
 
     def greet(device):
         pl.semaphore_signal(barrier, inc=1, device_id=device, device_id_type=MESH)
 
-    reach = (6, -6, 5, -5, 4, -4, 3, -3, 2, -2, 1, -1)
+    reach = (3, -3, 2, -2, 1, -1)
     for j in reach:
-        greet(at((z + j + NZ) % NZ, y, x, k))
+        greet(at(around(z + j, NZ), y, x, k))
     for j in range(1, NQ):
-        greet(plane((q + j) % NQ))
+        greet(plane(around(q + j, NQ)))
     greet(to_sib)
 
-    pairs = ((slot_hbm, slot_ref), (vals_hbm, vals_ref), (omega_hbm, omega_ref))
-    loads = [pltpu.make_async_copy(a, b, load_sem.at[i]) for i, (a, b) in enumerate(pairs)]
-    for load in loads:
-        load.start()
     for load in loads:
         load.wait()
 
@@ -144,13 +157,13 @@
     for b in range(slots):
         slot = slot_ref[0, b]
         on = count_ref[0, 0] > b
-        row_of.append(slot // col_blocks)
+        row_of.append(lax.div(slot, col_blocks))
         live.append(jnp.where(on, 1.0, 0.0).astype(F32))
-        picked = omega_ref[pl.ds(slot % col_blocks, 1)].reshape(BS, RANK)
+        picked = omega_ref[pl.ds(lax.rem(slot, col_blocks), 1)].reshape(BS, RANK)
         prods.append(jnp.dot(vals_ref[b], picked, preferred_element_type=F32))
         a_all[pl.ds(y, 1), b] = (vals_ref[b] * live[b].astype(jnp.bfloat16))[None]
         meta[pl.ds(y, 1), b] = jnp.full(
-            (1,) + meta.shape[2:], jnp.where(on, slot % col_blocks, -1), jnp.int32
+            (1,) + meta.shape[2:], jnp.where(on, lax.rem(slot, col_blocks), -1), jnp.int32
         )
 
     def fill(kk):
@@ -164,69 +177,87 @@
 
     fill(sib)
     pl.semaphore_wait(barrier, NQ + len(reach))
+    for j in (3, -3):
+        to = at(around(z + j, NZ), y, x, k)
+        pl.semaphore_signal(beyond_sem, inc=1, device_id=to, device_id_type=MESH)
 
     def sib_copy(xx):
         return copy(part.at[sib, xx], r1.at[xx], r1_sem.at[xx], to_sib)
 
-    def x_copy(d):
-        xx = (x + d) % NX
-        return copy(part.at[k, xx], r2.at[d - 1], r2_sem.at[d - 1], at(z, y, xx, k))
-
-    order = (2, 1, 3, 0)
-    for d in order:
-        go(sib_copy((x + d) % NX))
-    fill(k)
-    for d in order:
-        xx = (x + d) % NX
+    half = BS // 2
+    sides = (1, -1)
+
+    def rows_of(i):
+        return pl.ds(i * half, half)
+
+    def relay_copy(i):
+        src = part.at[k, around(x + 2, NX), rows_of(i)]
+        return copy(src, relay.at[i], relay_sem.at[i], at(z, y, around(x + sides[i], NX), k))
+
+    def x_copy(i, r):
+        xx = around(x + sides[i], NX)
+        src = part.at[k, xx, rows_of(r)]
+        return copy(src, r2.at[i, rows_of(r)], r2_sem.at[i, r], at(z, y, xx, k))
+
+    def a_copies(d):
+        to = at(z, around(y + d, NY), x, k)
+        return (
+            copy(a_all.at[y], a_all.at[y], a_sem.at[d - 1], to),
+            copy(meta.at[y], meta.at[y], m_sem.at[d - 1], to),
+        )
+
+    def join(d):
+        xx = around(x + d, NX)
         sib_copy(xx).wait_recv()
         part[pl.ds(k, 1), pl.ds(xx, 1)] = (
             part[pl.ds(k, 1), pl.ds(xx, 1)] + r1[pl.ds(xx, 1)][None]
         )
-        if d:
-            go(x_copy(d))
-
-    def a_copies(d):
-        to = at(z, (y + d) % NY, x, k)
-        return (
-            copy(a_all.at[y], a_all.at[y], a_sem.at[d - 1], to),
-            copy(meta.at[y], meta.at[y], m_sem.at[d - 1], to),
-        )
-
+
+    for d in (2, 1, 3, 0):
+        go(sib_copy(around(x + d, NX)))
+    fill(k)
+    join(2)
+    for i in range(2):
+        go(relay_copy(i))
+    for i in range(2):
+        join(sides[i])
+        go(x_copy(i, 1 - i))
+    join(0)
     for d in (2, 1, 3):
         for c in a_copies(d):
             go(c)
-    for d in (1, 3, 2):
-        x_copy(d).wait_recv()
-    own[...] = (
-        part[pl.ds(k, 1), pl.ds(x, 1)].reshape(BS, RANK) + r2[0] + r2[1] + r2[2]
-    )
+    for i in range(2):
+        relay_copy(i).wait_recv()
+        at_rows = (pl.ds(k, 1), pl.ds(around(x + sides[i], NX), 1), rows_of(i))
+        part[at_rows] = part[at_rows] + relay[i][None, None]
+        go(x_copy(i, i))
+    for i in range(2):
+        for r in range(2):
+            x_copy(i, r).wait_recv()
+    own[...] = part[pl.ds(k, 1), pl.ds(x, 1)].reshape(BS, RANK) + r2[0] + r2[1]
 
     def gram_half(u, rows):
-        n = rows.shape[0]
-        pair[u, pl.ds(k, 1), 0:n] = rows[None]
-        mine = pair.at[u, k, pl.ds(0, n)]
-        swap = copy(mine, mine, pair_sem.at[u], to_sib)
-        go(swap)
-        copy(mine, pair.at[u, sib, pl.ds(0, n)], pair_sem.at[u], to_sib).wait_recv()
+        pair = pairs[u]
+        pair[pl.ds(k, 1)] = rows[None]
+        go(copy(pair.at[k], pair.at[k], pair_sem.at[u], to_sib))
+        copy(pair.at[k], pair.at[sib], pair_sem.at[u], to_sib).wait_recv()
+        n = NK * rows.shape[0]
         lanes = pl.ds(pl.multiple_of(k * HALF, HALF), HALF)
-        term = None
-        for kk in range(NK):
-            one = lax.dot_general(
-                pair[u, kk, pl.ds(0, n), lanes], pair[u, kk, 0:n], (((0,), (0,)), ((), ())),
-                precision=HI, preferred_element_type=F32,
-            )
-            term = one if term is None else term + one
+        term = lax.dot_general(
+            pair[:, :, lanes].reshape(n, HALF), pair[...].reshape(n, RANK), (((0,), (0,)), ((), ())),
+            precision=HI, preferred_element_type=F32,
+        )
         g_send[u] = term.reshape(NQ, PIECE, RANK)
         for j in range(1, NQ):
-            qq = (q + j) % NQ
+            qq = around(q + j, NQ)
             go(copy(g_send.at[u, qq], g_recv.at[u, q], g_sem.at[u], plane(qq)))
         g_recv[u, pl.ds(q, 1)] = g_send[u, pl.ds(q, 1)]
 
     def arrived(buffer, sem):
         copy(buffer, buffer, sem, to_sib).wait_recv()
 
-    group, member = z // NG, z % NG
-    way, reach0 = member // 2 * 2 - 1, 4 - member * (3 - member)
+    group, member = lax.div(z, NG), lax.rem(z, NG)
+    way, reach0 = lax.div(member, 2) * 2 - 1, 4 - member * (3 - member)
 
     def reduce_plane(u):
         arrived(g_recv.at[u, pl.ds(0, NQ - 1)], g_sem.at[u])
@@ -236,7 +267,7 @@
         z_near[u, pl.ds(member, 1)] = total[None]
         mine = z_near.at[u, member]
         for j in range(1, NG):
-            near = group * NG + (member + j) % NG
+            near = group * NG + around(member + j, NG)
             go(copy(mine, mine, near_sem.at[u], at(near, y, x, k)))
 
     def reduce_near(u):
@@ -246,8 +277,10 @@
             total = total + z_near[u, i]
         z_far[u, pl.ds(group, 1)] = total[None]
         mine = z_far.at[u, group]
+        if u == 0:
+            pl.semaphore_wait(beyond_sem, 2)
         for j in (2, 1, 0):
-            far = (z + way * (reach0 + j) + NZ) % NZ
+            far = around(z + way * (reach0 + j), NZ)
             go(copy(mine, mine, far_sem.at[u], at(far, y, x, k)))
 
     def reduce_far(u):
@@ -258,9 +291,10 @@
         g_all[u, pl.ds(k, 1), pl.ds(q, 1)] = total[None, None]
         mine = g_all.at[u, k, q]
         for j in range(1, NQ):
-            go(copy(mine, mine, ag_sem.at[u], plane((q + j) % NQ)))
+            go(copy(mine, mine, ag_sem.at[u], plane(around(q + j, NQ))))
 
     def gather_plane(u):
+        flush()
         arrived(g_all.at[u, k, pl.ds(0, NQ - 1)], ag_sem.at[u])
         go(copy(g_all.at[u, k], g_all.at[u, k], half_sem.at[u], to_sib))
         copy(g_all.at[u, k], g_all.at[u, sib], half_sem.at[u], to_sib).wait_recv()
@@ -274,21 +308,25 @@
     def s_copy(d, i):
         rows = pl.ds(i * depth, depth)
         return copy(
-            own.at[rows], s_all.at[k, x, rows], s_sem.at[d - 1, i], at(z, y, (x + d) % NX, k)
+            own.at[rows], s_all.at[k, x, rows], s_sem.at[d - 1, i], at(z, y, around(x + d, NX), k)
         )
 
     def s_arrival(d, i):
         rows = pl.ds(i * depth, depth)
         return copy(
-            own.at[rows], s_all.at[k, (x + NX - d) % NX, rows], s_sem.at[d - 1, i], to_sib
-        )
+            own.at[rows], s_all.at[k, around(x - d, NX), rows], s_sem.at[d - 1, i], to_sib
+        )
+
+    early = slots // 2
 
     def pick_copy(d):
-        return copy(pick.at[y], pick.at[y], pick_sem.at[d - 1], at(z, (y + d) % NY, x, k))
+        mine = pick.at[y, pl.ds(0, early)] if d == 2 else pick.at[y]
+        return copy(mine, mine, pick_sem.at[d - 1], at(z, around(y + d, NY), x, k))
 
     def pick_arrival(d):
-        yy = (y + NY - d) % NY
-        return copy(pick.at[y], pick.at[yy], pick_sem.at[d - 1], at(z, yy, x, k))
+        yy = around(y - d, NY)
+        here = pick.at[yy, pl.ds(0, early)] if d == 2 else pick.at[yy]
+        return copy(here, here, pick_sem.at[d - 1], at(z, yy, x, k))
 
     s_all[pl.ds(k, 1), pl.ds(x, 1)] = own[...][None, None]
     reduce_plane(0)
@@ -304,11 +342,11 @@
     go(copy(s_all.at[k], s_all.at[k], sib_sem, to_sib))
     copy(s_all.at[k], s_all.at[sib], sib_sem, to_sib).wait_recv()
     for b in range(slots):
-        rows = s_all[pl.ds(row_of[b] % NK, 1), pl.ds(row_of[b] // NK, 1)]
+        rows = s_all[pl.ds(lax.rem(row_of[b], NK), 1), pl.ds(lax.div(row_of[b], NK), 1)]
         pick[pl.ds(y, 1), b] = rows.reshape(1, BS, RANK)
     gram[...] = gather_plane(0) * (1.0 / (BS * RB * NY * NZ))
 
-    for d in (1, 3):
+    for d in (1, 3, 2):
         go(pick_copy(d))
     inverse_factor(gram, linv)
 
@@ -317,34 +355,71 @@
             rows, linv[...], (((1,), (1,)), ((), ())), precision=HI, preferred_element_type=F32
         ).astype(jnp.bfloat16)
 
-    across = (y + 2) % NY
-    for b in range(slots):
-        ready[pl.ds(y, 1), b] = basis_rows(pick[pl.ds(y, 1), b].reshape(BS, RANK))[None]
-    go(copy(ready.at[y], ready.at[y], ready_sem, at(z, across, x, k)))
-    basis_ref[...] = basis_rows(own[...])
-
-    def products(yy, formed):
-        for b in range(slots):
-            if formed:
-                rows = ready[pl.ds(yy, 1), b].reshape(BS, RANK)
-            else:
-                rows = basis_rows(pick[pl.ds(yy, 1), b].reshape(BS, RANK))
-            block = a_all[pl.ds(yy, 1), b].reshape(BS, BS)
-            prod[pl.ds(yy, 1), b] = lax.dot_general(
-                block, rows, (((0,), (0,)), ((), ())), preferred_element_type=F32
-            )[None]
-
-    products(y, True)
-    for d in (1, 3, 2):
-        yy = (y + NY - d) % NY
-        to = at(z, yy, x, k)
-        copy(a_all.at[y], a_all.at[yy], a_sem.at[d - 1], to).wait_recv()
-        copy(meta.at[y], meta.at[yy], m_sem.at[d - 1], to).wait_recv()
-        if d == 2:
-            copy(ready.at[y], ready.at[yy], ready_sem, to).wait_recv()
-        else:
-            pick_arrival(d).wait_recv()
-        products(yy, d == 2)
+    def form(yy, lo, hi):
+        def one(b, carry):
+            rows = basis_rows(pick[pl.ds(yy, 1), pl.ds(b, 1)].reshape(BS, RANK))
+            ready[pl.ds(yy, 1), pl.ds(b, 1)] = rows[None, None]
+            return carry
+
+        lax.fori_loop(lo, hi, one, 0)
+
+    def products(yy):
+        def one(b, carry):
+            prod[pl.ds(yy, 1), pl.ds(b, 1)] = lax.dot_general(
+                a_all[pl.ds(yy, 1), pl.ds(b, 1)].reshape(BS, BS),
+                ready[pl.ds(yy, 1), pl.ds(b, 1)].reshape(BS, RANK),
+                (((0,), (0,)), ((), ())), preferred_element_type=F32,
+            )[None, None]
+            return carry
+
+        lax.fori_loop(0, slots, one, 0)
+
+    def ready_copy(yy):
+        late = pl.ds(early, slots - early)
+        to = at(z, around(y + 2, NY), x, k)
+        return copy(ready.at[yy, late], ready.at[yy, late], ready_sem, to)
+
+    def each(i, carry):
+        d = jnp.where(i == 3, 2, jnp.where(i == 2, 3, i))
+        yy = around(y - d, NY)
+
+        @pl.when(i > 0)
+        def _():
+            to = at(z, yy, x, k)
+            copy(a_all.at[y], a_all.at[yy], a_sem.at[d - 1], to).wait_recv()
+            copy(meta.at[y], meta.at[yy], m_sem.at[d - 1], to).wait_recv()
+
+        @pl.when((i == 1) | (i == 2))
+        def _():
+            copy(pick.at[y], pick.at[yy], pick_sem.at[d - 1], to_sib).wait_recv()
+
+        @pl.when(i == 3)
+        def _():
+            pick_arrival(2).wait_recv()
+
+        @pl.when(i < 3)
+        def _():
+            form(yy, early, slots)
+
+        @pl.when(i == 0)
+        def _():
+            ready_copy(y).start()
+
+        form(yy, 0, early)
+
+        @pl.when(i == 0)
+        def _():
+            basis_ref[...] = basis_rows(own[...])
+
+        @pl.when(i == 3)
+        def _():
+            ready_copy(yy).wait_recv()
+
+        products(yy)
+        return carry
+
+    lax.fori_loop(0, NY, each, 0)
+    pending.append(ready_copy(y).wait_send)
 
     tile = 16
     per_strip = STRIP // tile
@@ -360,7 +435,8 @@
         totals = []
         for t in range(per_strip):
             g = zz * (NY * per_strip) + y * per_strip + t
-            block, rows = g // (BS // tile), pl.multiple_of(g % (BS // tile) * tile, tile)
+            block = lax.div(g, BS // tile)
+            rows = pl.multiple_of(lax.rem(g, BS // tile) * tile, tile)
             total = jnp.zeros((tile, RANK), F32)
             for yy in range(NY):
                 for b in range(slots):
@@ -380,15 +456,15 @@
     near = (1, -1, 2)
 
     def w1_copy(i, e):
-        mid = (z + sign * near[i] + NZ) % NZ
-        dest = (mid + FAR[e] + NZ) % NZ
+        mid = around(z + sign * near[i], NZ)
+        dest = around(mid + FAR[e], NZ)
         return copy(code1.at[dest], w1.at[e, i], w1_sem.at[e, i], at(mid, y, x, k))
 
     def c1_copy(i):
-        return copy(unit1, c1.at[i], c1_sem.at[i], at((z + sign * near[i] + NZ) % NZ, y, x, k))
+        return copy(unit1, c1.at[i], c1_sem.at[i], at(around(z + sign * near[i], NZ), y, x, k))
 
     def w2_copies(e):
-        to = at((z + FAR[e] + NZ) % NZ, y, x, k)
+        to = at(around(z + FAR[e], NZ), y, x, k)
         return (
             copy(code2.at[e], w2.at[e], w2_sem.at[e], to),
             copy(unit2.at[e], c2.at[e], c2_sem.at[e], to),
@@ -404,7 +480,7 @@
     for e in range(4):
         for i in range(3):
             w1_copy(i, e).wait_recv()
-        dest = (z + FAR[e] + NZ) % NZ
+        dest = around(z + FAR[e], NZ)
         total = strip[pl.ds(dest, 1)].reshape(STRIP, RANK)
         for i in range(3):
             total = total + value(w1[e, i], c1[i, pl.ds(dest, 1), :])
@@ -425,8 +501,7 @@
     reduce_far(1)
     core_ref[...] = gather_plane(1) / float(col_blocks * BS * NX * NK)
 
-    for wait in pending:
-        wait()
+    flush()
 
 
 def body(block_vals, block_slot, block_count, omega):
@@ -454,14 +529,16 @@
             pltpu.VMEM((omega.shape[0] // BS, BS, RANK), omega.dtype),
             blocks(NK, NX),
             blocks(NX),
-            blocks(NX - 1),
+            pltpu.VMEM((2, BS // 2, RANK), F32),
+            blocks(2),
             blocks(),
             blocks(NK, NX),
             blocks(NY, slots),
             pltpu.VMEM((NY, slots, BS, RANK), jnp.bfloat16),
             pltpu.VMEM((NY, slots, BS, BS), jnp.bfloat16),
             pltpu.VMEM((NY, slots, 16, 128), jnp.int32),
-            blocks(2, NK),
+            blocks(NK),
+            pltpu.VMEM((NK, STRIP, RANK), F32),
             pltpu.VMEM((2, NQ, PIECE, RANK), F32),
             pltpu.VMEM((2, NQ, PIECE, RANK), F32),
             pltpu.VMEM((2, NG, PIECE, RANK), F32),
@@ -479,8 +556,9 @@
             pltpu.VMEM((3, NZ, RANK), F32),
             pltpu.VMEM((4, STRIP, RANK), jnp.int16),
             pltpu.VMEM((4, 1, RANK), F32),
+            pltpu.SemaphoreType.REGULAR,
             dma((3,)), dma,
-            dma((NX,)), dma((NX - 1,)), dma((NX - 1, 2)), dma, dma((NY - 1,)), dma((NY - 1,)), dma((NY - 1,)), dma,
+            dma((NX,)), dma((2,)), dma((2, 2)), dma((NX - 1, 2)), dma, dma((NY - 1,)), dma((NY - 1,)), dma((NY - 1,)), dma,
             dma((2,)), dma((2,)), dma((2,)), dma((2,)), dma((2,)), dma((2,)), dma((4, 3)), dma((3,)), dma((4,)), dma((4,)),
         ],
         compiler_params=pltpu.CompilerParams(

time: 103 us -> 98.7 us (0.958)
  Pallas kernels: 99.4 us -> 95.3 us
    pallas_call x1, Pallas kernels: 99.4 us -> 95.3 us  [body(): pl.pallas_call(kernel, out_shape=(pltpu.VMEM((BS, RANK), jnp.bfloat16), p...]
where the time goes in v3:
time: 98.7 us; the launch traced here: 98.6 us
  Pallas kernels  95.3 us (97%)
  local copies, waits for them, and re-layouts  1.95 us (2%)
  between operations  1.29 us (1%)
    pallas_call x1, Pallas kernels, body(): pl.pallas_call(kernel, out_shape=(pltpu.VMEM((BS, RANK), jnp.bfloat16), p...  95.3 us

profile of v3, /device:TPU:1, one launch (start us, length us, event | category | flops | bytes accessed | tf_op | source)
XLA Modules:
  0.0 98.6 jit_solution(166909329150295977)
XLA Ops:
  1.3 95.3 %range_basis.1 = (bf16[128,256]{1,0:T(8,128)(2,1)S(1)}, f32[1,48,256]{2,1,0:T(8,128)S(1)}, f32[256,256]{1,0:T(8,128)S(1)}) custom-call(bf16[2,128,128]{2,1,0:T(8,128)(2,1)} %vals_hbm.1, s32[1,2]{1,0:T(1,128)} %bitcast.3, bf16[24,128,256]{2,1,0:T(8,128)(2,1)} %bitcast.2, s32[1,1]{1,0:T(1,128)S(6)} %copy.13.count_ref), custom_call_target="tpu_custom_call" | custom-call | tf_op jit(solution)/shard_map/range_basis/pallas_call | solution.py:517
  96.6 0.6 copy.10
  97.2 0.6 copy.11
  97.9 0.7 copy.12

commit v4 on v3

--- a/solution.py
+++ b/solution.py
@@ -94,7 +94,7 @@
     vals_ref, slot_ref, omega_ref,
     part, r1, relay, r2, own, s_all, pick, ready, a_all, meta,
     pair0, pair1, g_send, g_recv, z_near, z_far, g_all,
-    gram, linv, prod, strip, code1, unit1, code2, unit2, w1, c1, w2, c2,
+    gram, linv, factor, prod, strip, code1, unit1, code2, unit2, w1, c1, w2, c2,
     beyond_sem, load_sem, send_sem, r1_sem, relay_sem, r2_sem, s_sem, sib_sem, a_sem, m_sem, pick_sem, ready_sem,
     pair_sem, g_sem, near_sem, far_sem, ag_sem, half_sem, w1_sem, c1_sem, w2_sem, c2_sem,
 ):
@@ -223,9 +223,6 @@
         join(sides[i])
         go(x_copy(i, 1 - i))
     join(0)
-    for d in (2, 1, 3):
-        for c in a_copies(d):
-            go(c)
     for i in range(2):
         relay_copy(i).wait_recv()
         at_rows = (pl.ds(k, 1), pl.ds(around(x + sides[i], NX), 1), rows_of(i))
@@ -317,16 +314,12 @@
             own.at[rows], s_all.at[k, around(x - d, NX), rows], s_sem.at[d - 1, i], to_sib
         )
 
-    early = slots // 2
-
     def pick_copy(d):
-        mine = pick.at[y, pl.ds(0, early)] if d == 2 else pick.at[y]
-        return copy(mine, mine, pick_sem.at[d - 1], at(z, around(y + d, NY), x, k))
+        return copy(pick.at[y], pick.at[y], pick_sem.at[d - 1], at(z, around(y + d, NY), x, k))
 
     def pick_arrival(d):
         yy = around(y - d, NY)
-        here = pick.at[yy, pl.ds(0, early)] if d == 2 else pick.at[yy]
-        return copy(here, here, pick_sem.at[d - 1], at(z, yy, x, k))
+        return copy(pick.at[y], pick.at[yy], pick_sem.at[d - 1], at(z, yy, x, k))
 
     s_all[pl.ds(k, 1), pl.ds(x, 1)] = own[...][None, None]
     reduce_plane(0)
@@ -335,6 +328,9 @@
     reduce_near(0)
     for d in (2, 1, 3):
         go(s_copy(d, 1))
+    for d in (2, 1, 3):
+        for c in a_copies(d):
+            go(c)
     reduce_far(0)
     for d in (1, 3, 2):
         for i in range(parts):
@@ -346,22 +342,52 @@
         pick[pl.ds(y, 1), b] = rows.reshape(1, BS, RANK)
     gram[...] = gather_plane(0) * (1.0 / (BS * RB * NY * NZ))
 
-    for d in (1, 3, 2):
+    for d in (1, 3):
         go(pick_copy(d))
     inverse_factor(gram, linv)
 
+    def split(v):
+        high = v.astype(jnp.bfloat16)
+        rest = v - high.astype(F32)
+        middle = rest.astype(jnp.bfloat16)
+        return high, middle, (rest - middle.astype(F32)).astype(jnp.bfloat16)
+
+    high, middle, low = split(linv[...].T)
+    for i, v in enumerate((high, high, high, middle, middle, low)):
+        factor[pl.ds(i * RANK, RANK), :] = v
+
     def basis_rows(rows):
-        return lax.dot_general(
-            rows, linv[...], (((1,), (1,)), ((), ())), precision=HI, preferred_element_type=F32
-        ).astype(jnp.bfloat16)
-
-    def form(yy, lo, hi):
-        def one(b, carry):
-            rows = basis_rows(pick[pl.ds(yy, 1), pl.ds(b, 1)].reshape(BS, RANK))
-            ready[pl.ds(yy, 1), pl.ds(b, 1)] = rows[None, None]
-            return carry
-
-        lax.fori_loop(lo, hi, one, 0)
+        high, middle, low = split(rows)
+        wide = jnp.concatenate([high, middle, low, high, middle, high], axis=1)
+        return jnp.dot(wide, factor[...], preferred_element_type=F32).astype(jnp.bfloat16)
+
+    before, after, across = around(y - 1, NY), around(y + 1, NY), around(y + 2, NY)
+    part0, part1 = pl.ds(0, slots // 2), pl.ds(slots // 2, slots - slots // 2)
+
+    def pass_on(i, yy):
+        blocks = (part0, part1)[i]
+        to = at(z, (after, before)[i], x, k)
+        return copy(ready.at[yy, blocks], ready.at[yy, blocks], ready_sem.at[i], to)
+
+    def form(*which):
+        rows = basis_rows(
+            jnp.concatenate([pick[pl.ds(yy, 1), b].reshape(b.size * BS, RANK) for yy, b in which])
+        )
+        at_row = 0
+        for yy, b in which:
+            ready[pl.ds(yy, 1), b] = rows[at_row : at_row + b.size * BS].reshape(
+                1, b.size, BS, RANK
+            )
+            at_row += b.size * BS
+
+    for d in (1, 3):
+        pick_arrival(d).wait_recv()
+    form((before, part0), (after, part1))
+    go(pass_on(0, before))
+    go(pass_on(1, after))
+    form((y, pl.ds(0, slots)))
+    form((before, part1), (after, part0))
+    basis_ref[...] = basis_rows(own[...])
 
     def products(yy):
         def one(b, carry):
@@ -374,52 +400,16 @@
 
         lax.fori_loop(0, slots, one, 0)
 
-    def ready_copy(yy):
-        late = pl.ds(early, slots - early)
-        to = at(z, around(y + 2, NY), x, k)
-        return copy(ready.at[yy, late], ready.at[yy, late], ready_sem, to)
-
-    def each(i, carry):
-        d = jnp.where(i == 3, 2, jnp.where(i == 2, 3, i))
+    products(y)
+    for d in (1, 3, 2):
         yy = around(y - d, NY)
-
-        @pl.when(i > 0)
-        def _():
-            to = at(z, yy, x, k)
-            copy(a_all.at[y], a_all.at[yy], a_sem.at[d - 1], to).wait_recv()
-            copy(meta.at[y], meta.at[yy], m_sem.at[d - 1], to).wait_recv()
-
-        @pl.when((i == 1) | (i == 2))
-        def _():
-            copy(pick.at[y], pick.at[yy], pick_sem.at[d - 1], to_sib).wait_recv()
-
-        @pl.when(i == 3)
-        def _():
-            pick_arrival(2).wait_recv()
-
-        @pl.when(i < 3)
-        def _():
-            form(yy, early, slots)
-
-        @pl.when(i == 0)
-        def _():
-            ready_copy(y).start()
-
-        form(yy, 0, early)
-
-        @pl.when(i == 0)
-        def _():
-            basis_ref[...] = basis_rows(own[...])
-
-        @pl.when(i == 3)
-        def _():
-            ready_copy(yy).wait_recv()
-
+        to = at(z, yy, x, k)
+        copy(a_all.at[y], a_all.at[yy], a_sem.at[d - 1], to).wait_recv()
+        copy(meta.at[y], meta.at[yy], m_sem.at[d - 1], to).wait_recv()
+        if d == 2:
+            pass_on(0, across).wait_recv()
+            pass_on(1, across).wait_recv()
         products(yy)
-        return carry
-
-    lax.fori_loop(0, NY, each, 0)
-    pending.append(ready_copy(y).wait_send)
 
     tile = 16
     per_strip = STRIP // tile
@@ -447,10 +437,9 @@
         strip[pl.ds(zz, 1)] = total[None]
         steps, unit = coded(total)
         code1[pl.ds(zz, 1)] = steps[None]
-        unit1[pl.ds(zz, 1), :] = unit
+        unit1[pl.ds(zz, 1)] = unit[None]
         return carry
 
-    lax.fori_loop(0, NZ, place, 0)
 
     sign = 1 - 2 * k
     near = (1, -1, 2)
@@ -460,8 +449,10 @@
         dest = around(mid + FAR[e], NZ)
         return copy(code1.at[dest], w1.at[e, i], w1_sem.at[e, i], at(mid, y, x, k))
 
-    def c1_copy(i):
-        return copy(unit1, c1.at[i], c1_sem.at[i], at(around(z + sign * near[i], NZ), y, x, k))
+    def c1_copy(i, e):
+        mid = around(z + sign * near[i], NZ)
+        dest = around(mid + FAR[e], NZ)
+        return copy(unit1.at[dest], c1.at[e, i], c1_sem.at[e, i], at(mid, y, x, k))
 
     def w2_copies(e):
         to = at(around(z + FAR[e], NZ), y, x, k)
@@ -470,20 +461,23 @@
             copy(unit2.at[e], c2.at[e], c2_sem.at[e], to),
         )
 
-    for i in (2, 0, 1):
-        go(c1_copy(i))
     for e in range(4):
+
+        def put(i, carry):
+            step = jnp.where(i == 3, 0, jnp.where(i == 2, 2, 1 - 2 * i))
+            return place(around(around(z + sign * step, NZ) + FAR[e], NZ), carry)
+
+        lax.fori_loop(0, 4, put, 0)
         for i in (2, 0, 1):
             go(w1_copy(i, e))
-    for i in range(3):
-        c1_copy(i).wait_recv()
+            go(c1_copy(i, e))
     for e in range(4):
-        for i in range(3):
-            w1_copy(i, e).wait_recv()
         dest = around(z + FAR[e], NZ)
         total = strip[pl.ds(dest, 1)].reshape(STRIP, RANK)
         for i in range(3):
-            total = total + value(w1[e, i], c1[i, pl.ds(dest, 1), :])
+            w1_copy(i, e).wait_recv()
+            c1_copy(i, e).wait_recv()
+            total = total + value(w1[e, i], c1[e, i])
         code2[e], unit2[e] = coded(total)
         for c in w2_copies(e):
             go(c)
@@ -546,20 +540,21 @@
             pltpu.VMEM((2, NK, NQ, PIECE, RANK), F32),
             pltpu.VMEM((RANK, RANK), F32),
             pltpu.VMEM((RANK, RANK), F32),
+            pltpu.VMEM((6 * RANK, RANK), jnp.bfloat16),
             blocks(NY, slots),
             pltpu.VMEM((NZ, STRIP, RANK), F32),
             pltpu.VMEM((NZ, STRIP, RANK), jnp.int16),
-            pltpu.VMEM((NZ, RANK), F32),
+            pltpu.VMEM((NZ, 1, RANK), F32),
             pltpu.VMEM((4, STRIP, RANK), jnp.int16),
             pltpu.VMEM((4, 1, RANK), F32),
             pltpu.VMEM((4, 3, STRIP, RANK), jnp.int16),
-            pltpu.VMEM((3, NZ, RANK), F32),
+            pltpu.VMEM((4, 3, 1, RANK), F32),
             pltpu.VMEM((4, STRIP, RANK), jnp.int16),
             pltpu.VMEM((4, 1, RANK), F32),
             pltpu.SemaphoreType.REGULAR,
             dma((3,)), dma,
-            dma((NX,)), dma((2,)), dma((2, 2)), dma((NX - 1, 2)), dma, dma((NY - 1,)), dma((NY - 1,)), dma((NY - 1,)), dma,
-            dma((2,)), dma((2,)), dma((2,)), dma((2,)), dma((2,)), dma((2,)), dma((4, 3)), dma((3,)), dma((4,)), dma((4,)),
+            dma((NX,)), dma((2,)), dma((2, 2)), dma((NX - 1, 2)), dma, dma((NY - 1,)), dma((NY - 1,)), dma((NY - 1,)), dma((2,)),
+            dma((2,)), dma((2,)), dma((2,)), dma((2,)), dma((2,)), dma((2,)), dma((4, 3)), dma((4, 3)), dma((4,)), dma((4,)),
         ],
         compiler_params=pltpu.CompilerParams(
             collective_id=0, has_side_effects=True, vmem_limit_bytes=60 * 2**20

time: 98.7 us -> 97.6 us (0.989)
  Pallas kernels: 95.3 us -> 94.2 us
    pallas_call x1, Pallas kernels: 95.3 us -> 94.2 us  [body(): pl.pallas_call(kernel, out_shape=(pltpu.VMEM((BS, RANK), jnp.bfloat16), p...]
where the time goes in v4:
time: 97.6 us; the launch traced here: 97.5 us
  Pallas kernels  94.2 us (97%)
  local copies, waits for them, and re-layouts  1.95 us (2%)
  between operations  1.29 us (1%)
    pallas_call x1, Pallas kernels, body(): pl.pallas_call(kernel, out_shape=(pltpu.VMEM((BS, RANK), jnp.bfloat16), p...  94.2 us
    unnamed x3, local copies, waits for them, and re-layouts  1.95 us

profile of v4, /device:TPU:1, one launch (start us, length us, event | category | flops | bytes accessed | tf_op | source)
XLA Modules:
  0.0 97.5 jit_solution(15729363533710518838)
XLA Ops:
  1.3 94.2 %range_basis.1 = (bf16[128,256]{1,0:T(8,128)(2,1)S(1)}, f32[1,48,256]{2,1,0:T(8,128)S(1)}, f32[256,256]{1,0:T(8,128)S(1)}) custom-call(bf16[2,128,128]{2,1,0:T(8,128)(2,1)} %vals_hbm.1, s32[1,2]{1,0:T(1,128)} %bitcast.3, bf16[24,128,256]{2,1,0:T(8,128)(2,1)} %bitcast.2, s32[1,1]{1,0:T(1,128)S(6)} %copy.13.count_ref), custom_call_target="tpu_custom_call" | custom-call | tf_op jit(solution)/shard_map/range_basis/pallas_call | solution.py:511
  95.5 0.6 copy.10
  96.2 0.6 copy.11
  96.8 0.7 copy.12

commit v5 on v4

--- a/solution.py
+++ b/solution.py
@@ -23,6 +23,13 @@
 NG = 4
 STEPS = 32767.0
 FAR = (6, -6, 2, -2)
+
+
+def split(v):
+    high = v.astype(jnp.bfloat16)
+    rest = v - high.astype(F32)
+    middle = rest.astype(jnp.bfloat16)
+    return high, middle, (rest - middle.astype(F32)).astype(jnp.bfloat16)
 
 
 def inverse_factor(a_ref, out_ref):
@@ -78,8 +85,11 @@
         def _():
             turned = pltpu.roll(done, n - PB, 1)
             rest = pltpu.roll(jnp.where(lane_rest < PB, 0.0, a_ref[PB:n, :]), n - PB, 1)
+            high, middle, low = split(turned)
             step = lax.dot_general(
-                turned, turned, (((0,), (0,)), ((), ())), precision=HI, preferred_element_type=F32
+                jnp.concatenate([high, middle, low, high, middle, high], axis=0),
+                jnp.concatenate([high, high, high, middle, middle, low], axis=0),
+                (((0,), (0,)), ((), ())), preferred_element_type=F32,
             )
             a_ref[0 : n - PB, :] = rest - step[0 : n - PB]
 
@@ -153,7 +163,7 @@
 
     col_blocks = omega_ref.shape[0]
     slots = vals_ref.shape[0]
-    row_of, live, prods = [], [], []
+    row_of, column, live, prods = [], [], [], []
     for b in range(slots):
         slot = slot_ref[0, b]
         on = count_ref[0, 0] > b
@@ -161,21 +171,16 @@
         live.append(jnp.where(on, 1.0, 0.0).astype(F32))
         picked = omega_ref[pl.ds(lax.rem(slot, col_blocks), 1)].reshape(BS, RANK)
         prods.append(jnp.dot(vals_ref[b], picked, preferred_element_type=F32))
-        a_all[pl.ds(y, 1), b] = (vals_ref[b] * live[b].astype(jnp.bfloat16))[None]
-        meta[pl.ds(y, 1), b] = jnp.full(
-            (1,) + meta.shape[2:], jnp.where(on, lax.rem(slot, col_blocks), -1), jnp.int32
-        )
-
-    def fill(kk):
-        for xx in range(NX):
-            block = xx * NK + kk
-            total = None
-            for b in range(slots):
-                term = prods[b] * (jnp.where(row_of[b] == block, 1.0, 0.0).astype(F32) * live[b])
-                total = term if total is None else total + term
-            part[pl.ds(kk, 1), xx] = total[None]
-
-    fill(sib)
+        column.append(jnp.where(on, lax.rem(slot, col_blocks), -1))
+
+    def fill(kk, xx):
+        total = None
+        for b in range(slots):
+            here = row_of[b] == xx * NK + kk
+            term = prods[b] * (jnp.where(here, 1.0, 0.0).astype(F32) * live[b])
+            total = term if total is None else total + term
+        part[pl.ds(kk, 1), pl.ds(xx, 1)] = total[None, None]
+
     pl.semaphore_wait(barrier, NQ + len(reach))
     for j in (3, -3):
         to = at(around(z + j, NZ), y, x, k)
@@ -214,8 +219,14 @@
         )
 
     for d in (2, 1, 3, 0):
-        go(sib_copy(around(x + d, NX)))
-    fill(k)
+        xx = around(x + d, NX)
+        fill(sib, xx)
+        go(sib_copy(xx))
+    for xx in range(NX):
+        fill(k, xx)
+    for b in range(slots):
+        a_all[pl.ds(y, 1), b] = (vals_ref[b] * live[b].astype(jnp.bfloat16))[None]
+        meta[pl.ds(y, 1), b] = jnp.full((1,) + meta.shape[2:], column[b], jnp.int32)
     join(2)
     for i in range(2):
         go(relay_copy(i))
@@ -285,6 +296,7 @@
         total = z_far[u, 0]
         for i in range(1, NZ // NG):
             total = total + z_far[u, i]
+        total = total * (1.0 / (BS * RB * NY * NZ) if u == 0 else 1.0 / (col_blocks * BS * NX * NK))
         g_all[u, pl.ds(k, 1), pl.ds(q, 1)] = total[None, None]
         mine = g_all.at[u, k, q]
         for j in range(1, NQ):
@@ -340,17 +352,11 @@
     for b in range(slots):
         rows = s_all[pl.ds(lax.rem(row_of[b], NK), 1), pl.ds(lax.div(row_of[b], NK), 1)]
         pick[pl.ds(y, 1), b] = rows.reshape(1, BS, RANK)
-    gram[...] = gather_plane(0) * (1.0 / (BS * RB * NY * NZ))
+    gram[...] = gather_plane(0)
 
     for d in (1, 3):
         go(pick_copy(d))
     inverse_factor(gram, linv)
-
-    def split(v):
-        high = v.astype(jnp.bfloat16)
-        rest = v - high.astype(F32)
-        middle = rest.astype(jnp.bfloat16)
-        return high, middle, (rest - middle.astype(F32)).astype(jnp.bfloat16)
 
     high, middle, low = split(linv[...].T)
     for i, v in enumerate((high, high, high, middle, middle, low)):
@@ -493,7 +499,7 @@
     reduce_plane(1)
     reduce_near(1)
     reduce_far(1)
-    core_ref[...] = gather_plane(1) / float(col_blocks * BS * NX * NK)
+    core_ref[...] = gather_plane(1)
 
     flush()
 

time: 97.6 us -> 97.1 us (level)
  no operation moved by 1% of the time
where the time goes in v5:
time: 97.1 us; the launch traced here: 97 us
  Pallas kernels  93.7 us (96%)
  local copies, waits for them, and re-layouts  1.95 us (2%)
  between operations  1.29 us (1%)
    pallas_call x1, Pallas kernels, body(): pl.pallas_call(kernel, out_shape=(pltpu.VMEM((BS, RANK), jnp.bfloat16), p...  93.7 us
    unnamed x3, local copies, waits for them, and re-layouts  1.95 us

profile of v5, /device:TPU:1, one launch (start us, length us, event | category | flops | bytes accessed | tf_op | source)
XLA Modules:
  0.0 97.0 jit_solution(9918407669782269532)
XLA Ops:
  1.3 93.7 %range_basis.1 = (bf16[128,256]{1,0:T(8,128)(2,1)S(1)}, f32[1,48,256]{2,1,0:T(8,128)S(1)}, f32[256,256]{1,0:T(8,128)S(1)}) custom-call(bf16[2,128,128]{2,1,0:T(8,128)(2,1)} %vals_hbm.1, s32[1,2]{1,0:T(1,128)} %bitcast.3, bf16[24,128,256]{2,1,0:T(8,128)(2,1)} %bitcast.2, s32[1,1]{1,0:T(1,128)S(6)} %copy.13.count_ref), custom_call_target="tpu_custom_call" | custom-call | tf_op jit(solution)/shard_map/range_basis/pallas_call | solution.py:517
  95.0 0.6 copy.10
  95.6 0.6 copy.11
  96.2 0.7 copy.12

commit v6 on v5

--- a/solution.py
+++ b/solution.py
@@ -251,9 +251,12 @@
         copy(pair.at[k], pair.at[sib], pair_sem.at[u], to_sib).wait_recv()
         n = NK * rows.shape[0]
         lanes = pl.ds(pl.multiple_of(k * HALF, HALF), HALF)
+        high, middle, low = split(pair[:, :, lanes].reshape(n, HALF))
+        left = jnp.concatenate([high, middle, low, high, middle, high], axis=0)
+        high, middle, low = split(pair[...].reshape(n, RANK))
+        right = jnp.concatenate([high, high, high, middle, middle, low], axis=0)
         term = lax.dot_general(
-            pair[:, :, lanes].reshape(n, HALF), pair[...].reshape(n, RANK), (((0,), (0,)), ((), ())),
-            precision=HI, preferred_element_type=F32,
+            left, right, (((0,), (0,)), ((), ())), preferred_element_type=F32
         )
         g_send[u] = term.reshape(NQ, PIECE, RANK)
         for j in range(1, NQ):

time: 97.1 us -> 97 us (level)
  no operation moved by 1% of the time
where the time goes in v6:
time: 97 us; the launch traced here: 96.9 us
  Pallas kernels  93.7 us (97%)
  local copies, waits for them, and re-layouts  1.95 us (2%)
  between operations  1.29 us (1%)
    pallas_call x1, Pallas kernels, body(): pl.pallas_call(kernel, out_shape=(pltpu.VMEM((BS, RANK), jnp.bfloat16), p...  93.7 us
    unnamed x3, local copies, waits for them, and re-layouts  1.95 us

profile of v6, /device:TPU:1, one launch (start us, length us, event | category | flops | bytes accessed | tf_op | source)
XLA Modules:
  0.0 96.9 jit_solution(9363625228334105158)
XLA Ops:
  1.3 93.7 %range_basis.1 = (bf16[128,256]{1,0:T(8,128)(2,1)S(1)}, f32[1,48,256]{2,1,0:T(8,128)S(1)}, f32[256,256]{1,0:T(8,128)S(1)}) custom-call(bf16[2,128,128]{2,1,0:T(8,128)(2,1)} %vals_hbm.1, s32[1,2]{1,0:T(1,128)} %bitcast.3, bf16[24,128,256]{2,1,0:T(8,128)(2,1)} %bitcast.2, s32[1,1]{1,0:T(1,128)S(6)} %copy.13.count_ref), custom_call_target="tpu_custom_call" | custom-call | tf_op jit(solution)/shard_map/range_basis/pallas_call | solution.py:520
  94.9 0.6 copy.10
  95.6 0.6 copy.11
  96.2 0.7 copy.12
